TPU v7x, 512 devices: a whole 4x4x16 slice. The times are simulated.
512 devices in a mesh: gx: 4 (over y), gy: 4 (over x), gz: 32 (over z, core).
Axes of the slice: x: 4, y: 4, z: 16, core: 2. Of those that a mesh axis runs over, the one named last changes fastest.
Arguments:
- multipoles: float32 [121, 524288], P(None, ('gx', 'gy', 'gz')), may hold values from -6 to 6
- sources: int32 [16384, 1024], P(('gx', 'gy', 'gz')), may hold values from 0 to 2559
- halo_cells: int32 [3072, 256], P(('gx', 'gy', 'gz')), may hold values from 0 to 1023
- m2l_ops: float32 [32, 121, 121], replicated, may hold values from -0.09375 to 0.09375
- cell_up: float32 [8, 121, 121], replicated, may hold values from -0.015625 to 0.015625
- cell_down: float32 [8, 121, 121], replicated, may hold values from -0.5 to 0.5
- side_ops: float32 [3, 2, 121, 121], replicated, may hold values from -0.375 to 0.375
Outputs:
- local_fields: float32 [121, 524288], P(None, ('gx', 'gy', 'gz'))
Inputs may be any that keep to these rules, and one draw needn't show every extreme that they name: `sources`: slot of a device's own cells or its received face cells.
All inputs are finite; a program needn't handle non-finite values.
Results may differ from a plain program's by a relative error of at most 0.0003.
Values sent between devices are 32-bit elements; how exact they have to be, the bound alone decides.
A program may use at most 64 MiB of HBM per device.

v0:
```python
import jax
import jax.numpy as jnp
from jax import lax
from jax.sharding import PartitionSpec as P

HIGHEST = lax.Precision.HIGHEST


def extended(cells, sides, width):
    for axis, dim in sides:
        count = lax.axis_size(axis)
        ends = count - 1
        head = lax.slice_in_dim(cells, 0, width, axis=dim)
        tail = lax.slice_in_dim(cells, cells.shape[dim] - width, cells.shape[dim], axis=dim)
        cells = jnp.concatenate(
            [
                lax.ppermute(tail, axis, [(i, (i + 1) % count) for i in range(ends)]),
                cells,
                lax.ppermute(head, axis, [((i + 1) % count, i) for i in range(ends)]),
            ],
            axis=dim,
        )
    return cells


def from_partner(shard, axis, bit):
    return lax.ppermute(shard, axis, [(i, i ^ 1 << bit) for i in range(lax.axis_size(axis))])


def matvec(matrix, vector):
    return jnp.dot(matrix, vector, precision=HIGHEST)


def face_pair(multipoles, halo_cells, axis_number):
    lower_face = jnp.take(multipoles, halo_cells[2 * axis_number], axis=1)
    upper_face = jnp.take(multipoles, halo_cells[2 * axis_number + 1], axis=1)
    return jnp.stack([lower_face, upper_face])


def shards(multipoles, sources, halo_cells, m2l_ops, cell_up, cell_down, side_ops):
    num_coef, cells = multipoles.shape
    extended_x = extended(face_pair(multipoles, halo_cells, 0), (("gx", 0),), 1)
    extended_y = extended(face_pair(multipoles, halo_cells, 1), (("gy", 0),), 1)
    extended_z = extended(face_pair(multipoles, halo_cells, 2), (("gz", 0),), 1)
    source_pool = jnp.concatenate(
        [
            multipoles,
            extended_x[0],
            extended_x[3],
            extended_y[0],
            extended_y[3],
            extended_z[0],
            extended_z[3],
        ],
        axis=1,
    )
    pool_rows = jnp.transpose(source_pool)
    group = 8
    per_op = sources.shape[1]
    ops_groups = jnp.transpose(
        m2l_ops.reshape(-1, group, num_coef, num_coef), (0, 2, 1, 3)
    ).reshape(-1, num_coef, group * num_coef)
    source_groups = jnp.transpose(sources.reshape(-1, group, per_op), (0, 2, 1))

    def add_group(carry, items):
        ops_block, source_block = items
        picked = jnp.take(pool_rows, source_block, axis=0).reshape(per_op, group * num_coef)
        term = lax.dot_general(ops_block, picked, (((1,), (1,)), ((), ())), precision=HIGHEST)
        return (carry + term, None)

    near_field, unused = lax.scan(
        add_group, jnp.zeros((num_coef, cells), jnp.float32), (ops_groups, source_groups)
    )
    class_sums = multipoles.reshape(num_coef, cells // 8, 8).sum(axis=1)
    own_value = jnp.einsum("ocd,do->c", cell_up, class_sums, precision=HIGHEST)
    position = lax.axis_index(("gx", "gy", "gz"))
    depth = lax.axis_size(("gx", "gy", "gz")).bit_length() - 1
    far_list = []
    for level_bit in range(depth):
        partner = from_partner(own_value, ("gx", "gy", "gz"), level_bit)
        side_bit = position // 2**level_bit % 2
        far_list.append(matvec(side_ops[1, side_bit], partner))
        lower_half = jnp.where(side_bit == 0, own_value, partner)
        upper_half = jnp.where(side_bit == 0, partner, own_value)
        own_value = matvec(side_ops[0, 0], lower_half) + matvec(side_ops[0, 1], upper_half)
    local_field = jnp.zeros((num_coef,), jnp.float32)
    for level_bit in reversed(range(depth)):
        side_bit = position // 2**level_bit % 2
        local_field = matvec(side_ops[2, side_bit], local_field) + far_list[level_bit]
    shifted = jnp.einsum("ocd,d->co", cell_down, local_field, precision=HIGHEST)
    spread = jnp.broadcast_to(shifted[:, None, :], (num_coef, cells // 8, 8)).reshape(
        num_coef, cells
    )
    return near_field + spread


def solution(mesh):
    placed = (
        P(None, ("gx", "gy", "gz")),
        P(("gx", "gy", "gz"), None),
        P(("gx", "gy", "gz"), None),
        P(),
        P(),
        P(),
        P(),
    )
    return jax.shard_map(
        shards, mesh=mesh, in_specs=placed, out_specs=P(None, ("gx", "gy", "gz")), check_vma=False
    )
```

profile of v0, /device:TPU:480, one launch (start us, length us, event | category | flops | bytes accessed | tf_op | source)
XLA Modules:
  0.0 306.0 jit_solution(9552025776685316380)
XLA Ops:
  0.0 1.3 copy.131
  2.0 1.9 collective-permute-start.6
  5.5 4.1 %collective-permute-start = (f32[1,121,256]{1,2,0:T(8,128)}, f32[1,121,256]{1,2,0:T(8,128)}, u32[]{:S(2)}, u32[]{:S(2)}) collective-permute-start(f32[1,121,256]{1,2,0:T(8,128)} %select_bitcast_fusion.5), channel_id=1, source_target_pairs={{0,128},{128,256},{256,384},{1,129},{129,257},{257,385},{2,130},{1... | collective-permute-start | bytes 371720 | tf_op jit(solution)/shard_map/ppermute | solution.py:17
  11.1 1.3 collective-permute-start.1
  13.9 4.0 %collective-permute-start.2 = (f32[1,121,256]{1,2,0:T(8,128)}, f32[1,121,256]{1,2,0:T(8,128)}, u32[]{:S(2)}, u32[]{:S(2)}) collective-permute-start(f32[1,121,256]{1,2,0:T(8,128)} %select_bitcast_fusion.3), channel_id=1, source_target_pairs={{0,32},{32,64},{64,96},{1,33},{33,65},{65,97},{2,34},{34,66},{66,9... | collective-permute-start | bytes 371720 | tf_op jit(solution)/shard_map/ppermute | solution.py:17
  21.0 1.9 constant_dynamic-slice_fusion.1
  23.3 3.0 collective-permute-start.7
  26.3 2.5 collective-permute-done.7
  29.2 3.4 %collective-permute-start.8 = (f32[121]{0:T(128)S(1)}, f32[121]{0:T(128)S(1)}, u32[]{:S(2)}, u32[]{:S(2)}) collective-permute-start(f32[121]{0:T(128)S(1)} %fusion.24), channel_id=1, source_target_pairs={{0,4},{1,5},{2,6},{3,7},{4,0},{5,1},{6,2},{7,3},{8,12},{9,13},{10,... | collective-permute-start | bytes 1460 | tf_op jit(solution)/shard_map/ppermute | solution.py:27
  32.6 2.9 collective-permute-done.8
  36.0 5.5 %collective-permute-start.9 = (f32[121]{0:T(128)S(1)}, f32[121]{0:T(128)S(1)}, u32[]{:S(2)}, u32[]{:S(2)}) collective-permute-start(f32[121]{0:T(128)S(1)} %fusion.23), channel_id=1, source_target_pairs={{0,8},{1,9},{2,10},{3,11},{4,12},{5,13},{6,14},{7,15},{8,0},{9,1},... | collective-permute-start | bytes 1460 | tf_op jit(solution)/shard_map/ppermute | solution.py:27
  42.2 3.1 %collective-permute-done.9 = f32[121]{0:T(128)S(1)} collective-permute-done((f32[121]{0:T(128)S(1)}, f32[121]{0:T(128)S(1)}, u32[]{:S(2)}, u32[]{:S(2)}) %collective-permute-start.9) | collective-permute-done | bytes 516 | tf_op jit(solution)/shard_map/ppermute | solution.py:27
  45.8 6.4 %collective-permute-start.10 = (f32[121]{0:T(128)S(1)}, f32[121]{0:T(128)S(1)}, u32[]{:S(2)}, u32[]{:S(2)}) collective-permute-start(f32[121]{0:T(128)S(1)} %fusion.22), channel_id=1, source_target_pairs={{0,16},{1,17},{2,18},{3,19},{4,20},{5,21},{6,22},{7,23},{8,24},{9,... | collective-permute-start | bytes 1460 | tf_op jit(solution)/shard_map/ppermute | solution.py:27
  52.9 7.0 %collective-permute-done.10 = f32[121]{0:T(128)S(1)} collective-permute-done((f32[121]{0:T(128)S(1)}, f32[121]{0:T(128)S(1)}, u32[]{:S(2)}, u32[]{:S(2)}) %collective-permute-start.10) | collective-permute-done | bytes 516 | tf_op jit(solution)/shard_map/ppermute | solution.py:27
  60.3 4.6 %collective-permute-start.11 = (f32[121]{0:T(128)S(1)}, f32[121]{0:T(128)S(1)}, u32[]{:S(2)}, u32[]{:S(2)}) collective-permute-start(f32[121]{0:T(128)S(1)} %fusion.21), channel_id=1, source_target_pairs={{0,32},{1,33},{2,34},{3,35},{4,36},{5,37},{6,38},{7,39},{8,40},{9,... | collective-permute-start | bytes 1460 | tf_op jit(solution)/shard_map/ppermute | solution.py:27
  66.9 4.9 %collective-permute-start.12 = (f32[121]{0:T(128)S(1)}, f32[121]{0:T(128)S(1)}, u32[]{:S(2)}, u32[]{:S(2)}) collective-permute-start(f32[121]{0:T(128)S(1)} %fusion.20), channel_id=1, source_target_pairs={{0,64},{1,65},{2,66},{3,67},{4,68},{5,69},{6,70},{7,71},{8,72},{9,... | collective-permute-start | bytes 1460 | tf_op jit(solution)/shard_map/ppermute | solution.py:27
  72.5 1.4 collective-permute-done.12
  74.2 4.6 %collective-permute-start.13 = (f32[121]{0:T(128)S(1)}, f32[121]{0:T(128)S(1)}, u32[]{:S(2)}, u32[]{:S(2)}) collective-permute-start(f32[121]{0:T(128)S(1)} %fusion.19), channel_id=1, source_target_pairs={{0,128},{1,129},{2,130},{3,131},{4,132},{5,133},{6,134},{7,135},{8... | collective-permute-start | bytes 1460 | tf_op jit(solution)/shard_map/ppermute | solution.py:27
  78.9 1.4 collective-permute-done.13
  80.7 4.9 %collective-permute-start.14 = (f32[121]{0:T(128)S(1)}, f32[121]{0:T(128)S(1)}, u32[]{:S(2)}, u32[]{:S(2)}) collective-permute-start(f32[121]{0:T(128)S(1)} %fusion.18), channel_id=1, source_target_pairs={{0,256},{1,257},{2,258},{3,259},{4,260},{5,261},{6,262},{7,263},{8... | collective-permute-start | bytes 1460 | tf_op jit(solution)/shard_map/ppermute | solution.py:27
  86.0 4.1 %copy.124 = f32[4,8,121,121]{2,0,3,1:T(4,128)} copy(f32[4,8,121,121]{3,1,0,2:T(8,128)} %bitcast.391) | data formatting | bytes 3748096 | tf_op jit(solution)/shard_map/reshape | solution.py:61
  90.1 2.0 collective-permute-start.4
  96.6 3.8 %collective-permute-start.5 = (f32[1,121,256]{1,2,0:T(8,128)S(1)}, f32[1,121,256]{1,2,0:T(8,128)S(1)}, u32[]{:S(2)}, u32[]{:S(2)}) collective-permute-start(f32[1,121,256]{1,2,0:T(8,128)S(1)} %copy-done.11), channel_id=1, source_target_pairs={{1,0},{2,1},{3,2},{4,3},{5,4},{6,5},{7,6},{8,7},{9,8},{10,9},{11,1... | collective-permute-start | bytes 371720 | tf_op jit(solution)/shard_map/ppermute | solution.py:19
  104.2 200.5 %while.11 = (s32[]{:T(128)}, f32[121,1024]{1,0:T(8,128)S(1)}, f32[4,121,968]{1,0,2:T(4,128)}, s32[4,1024,8]{1,2,0:T(8,128)S(1)}, f32[2560,121]{1,0:T(8,128)S(1)}, /*index=5*/s32[]{:T(128)}, s32[]{:T(128)}) while((s32[]{:T(128)}, f32[121,1024]{1,0:T(8,128)S(1)}, f32[4,121,968]{1,0,2:T(4,128)}, s32[4,1024,8]{1,2,0:T(8,128)S(1)}, ...), condition=%wide.region_1.3_spmd.clone, body=%wide.region_0.0_spmd.clone.sunk | while | flops 1440589824 | bytes 38425280 | solution.py:71
  104.7 27.9 %gather_fusion = f32[8192,121]{1,0:T(8,128)} fusion(f32[2560,121]{1,0:T(8,128)S(1)} %get-tuple-element.169, s32[8192]{0:T(1024)S(1)} %broadcast_clamp_fusion.2), kind=kCustom, calls=%fused_computation.1.clone.clone.1 | custom fusion | bytes 7962624 | tf_op jit(solution)/shard_map/while/body/eval_jaxpr/jit(_take)/gather | solution.py:67
  132.5 5.5 %copy.242 = f32[1024,8,121]{0,2,1:T(8,128)} copy(f32[1024,8,121]{2,1,0:T(8,128)} %bitcast.388) | data formatting | bytes 7929856 | tf_op jit(solution)/shard_map/while/body/eval_jaxpr/jit(_take)/gather | solution.py:67
  138.0 5.1 %broadcast_select_fusion.18 = f32[1024,8,121]{0,2,1:T(8,128)} fusion(f32[1024,8,121]{0,2,1:T(8,128)} %copy.242, pred[1024,8]{0,1:T(8,128)(4,1)S(1)} %compare_and_fusion.8), kind=kLoop, calls=%fused_computation.7.clone.1 | loop fusion | flops 991232 | bytes 7938048 | tf_op jit(solution)/shard_map/while/body/eval_jaxpr/jit(_take)/select_n | solution.py:67
  143.2 4.5 %select_n.493 = f32[1024,968]{0,1:T(8,128)} reshape(f32[1024,8,121]{0,2,1:T(8,128)} %broadcast_select_fusion.18) | data formatting | bytes 7929856 | tf_op jit(solution)/shard_map/while/body/eval_jaxpr/jit(_take)/select_n | solution.py:67
  147.7 2.0 constant_dynamic-slice_fusion.20
  149.7 4.6 %convolution_add_fusion.2 = f32[121,1024]{1,0:T(8,128)S(1)} fusion(f32[121,968]{0,1:T(8,128)S(1)} %bitcast.389, f32[1024,968]{0,1:T(8,128)} %select_n.493, f32[121,1024]{1,0:T(8,128)S(1)} %get-tuple-element.159, pred[]{:T(512)S(6)} %compare.29), kind=kOutput, calls=%fused_computation.8.clone.1 | convolution fusion | flops 1439516672 | bytes 5424673 | tf_op jit(solution)/shard_map/while/body/eval_jaxpr/dot_general | solution.py:68
  154.8 27.9 %gather_fusion = f32[8192,121]{1,0:T(8,128)} fusion(f32[2560,121]{1,0:T(8,128)S(1)} %get-tuple-element.169, s32[8192]{0:T(1024)S(1)} %broadcast_clamp_fusion.2), kind=kCustom, calls=%fused_computation.1.clone.clone.1 | custom fusion | bytes 7962624 | tf_op jit(solution)/shard_map/while/body/eval_jaxpr/jit(_take)/gather | solution.py:67
  182.7 5.5 %copy.242 = f32[1024,8,121]{0,2,1:T(8,128)} copy(f32[1024,8,121]{2,1,0:T(8,128)} %bitcast.388) | data formatting | bytes 7929856 | tf_op jit(solution)/shard_map/while/body/eval_jaxpr/jit(_take)/gather | solution.py:67
  188.2 5.1 %broadcast_select_fusion.18 = f32[1024,8,121]{0,2,1:T(8,128)} fusion(f32[1024,8,121]{0,2,1:T(8,128)} %copy.242, pred[1024,8]{0,1:T(8,128)(4,1)S(1)} %compare_and_fusion.8), kind=kLoop, calls=%fused_computation.7.clone.1 | loop fusion | flops 991232 | bytes 7938048 | tf_op jit(solution)/shard_map/while/body/eval_jaxpr/jit(_take)/select_n | solution.py:67
  193.3 4.5 %select_n.493 = f32[1024,968]{0,1:T(8,128)} reshape(f32[1024,8,121]{0,2,1:T(8,128)} %broadcast_select_fusion.18) | data formatting | bytes 7929856 | tf_op jit(solution)/shard_map/while/body/eval_jaxpr/jit(_take)/select_n | solution.py:67
  197.8 2.0 constant_dynamic-slice_fusion.20
  199.8 4.6 %convolution_add_fusion.2 = f32[121,1024]{1,0:T(8,128)S(1)} fusion(f32[121,968]{0,1:T(8,128)S(1)} %bitcast.389, f32[1024,968]{0,1:T(8,128)} %select_n.493, f32[121,1024]{1,0:T(8,128)S(1)} %get-tuple-element.159, pred[]{:T(512)S(6)} %compare.29), kind=kOutput, calls=%fused_computation.8.clone.1 | convolution fusion | flops 1439516672 | bytes 5424673 | tf_op jit(solution)/shard_map/while/body/eval_jaxpr/dot_general | solution.py:68
  204.9 27.9 %gather_fusion = f32[8192,121]{1,0:T(8,128)} fusion(f32[2560,121]{1,0:T(8,128)S(1)} %get-tuple-element.169, s32[8192]{0:T(1024)S(1)} %broadcast_clamp_fusion.2), kind=kCustom, calls=%fused_computation.1.clone.clone.1 | custom fusion | bytes 7962624 | tf_op jit(solution)/shard_map/while/body/eval_jaxpr/jit(_take)/gather | solution.py:67
  232.8 5.5 %copy.242 = f32[1024,8,121]{0,2,1:T(8,128)} copy(f32[1024,8,121]{2,1,0:T(8,128)} %bitcast.388) | data formatting | bytes 7929856 | tf_op jit(solution)/shard_map/while/body/eval_jaxpr/jit(_take)/gather | solution.py:67
  238.3 5.1 %broadcast_select_fusion.18 = f32[1024,8,121]{0,2,1:T(8,128)} fusion(f32[1024,8,121]{0,2,1:T(8,128)} %copy.242, pred[1024,8]{0,1:T(8,128)(4,1)S(1)} %compare_and_fusion.8), kind=kLoop, calls=%fused_computation.7.clone.1 | loop fusion | flops 991232 | bytes 7938048 | tf_op jit(solution)/shard_map/while/body/eval_jaxpr/jit(_take)/select_n | solution.py:67
  243.4 4.5 %select_n.493 = f32[1024,968]{0,1:T(8,128)} reshape(f32[1024,8,121]{0,2,1:T(8,128)} %broadcast_select_fusion.18) | data formatting | bytes 7929856 | tf_op jit(solution)/shard_map/while/body/eval_jaxpr/jit(_take)/select_n | solution.py:67
  248.0 2.0 constant_dynamic-slice_fusion.20
  250.0 4.6 %convolution_add_fusion.2 = f32[121,1024]{1,0:T(8,128)S(1)} fusion(f32[121,968]{0,1:T(8,128)S(1)} %bitcast.389, f32[1024,968]{0,1:T(8,128)} %select_n.493, f32[121,1024]{1,0:T(8,128)S(1)} %get-tuple-element.159, pred[]{:T(512)S(6)} %compare.29), kind=kOutput, calls=%fused_computation.8.clone.1 | convolution fusion | flops 1439516672 | bytes 5424673 | tf_op jit(solution)/shard_map/while/body/eval_jaxpr/dot_general | solution.py:68
  255.1 27.9 %gather_fusion = f32[8192,121]{1,0:T(8,128)} fusion(f32[2560,121]{1,0:T(8,128)S(1)} %get-tuple-element.169, s32[8192]{0:T(1024)S(1)} %broadcast_clamp_fusion.2), kind=kCustom, calls=%fused_computation.1.clone.clone.1 | custom fusion | bytes 7962624 | tf_op jit(solution)/shard_map/while/body/eval_jaxpr/jit(_take)/gather | solution.py:67
  282.9 5.5 %copy.242 = f32[1024,8,121]{0,2,1:T(8,128)} copy(f32[1024,8,121]{2,1,0:T(8,128)} %bitcast.388) | data formatting | bytes 7929856 | tf_op jit(solution)/shard_map/while/body/eval_jaxpr/jit(_take)/gather | solution.py:67
  288.4 5.1 %broadcast_select_fusion.18 = f32[1024,8,121]{0,2,1:T(8,128)} fusion(f32[1024,8,121]{0,2,1:T(8,128)} %copy.242, pred[1024,8]{0,1:T(8,128)(4,1)S(1)} %compare_and_fusion.8), kind=kLoop, calls=%fused_computation.7.clone.1 | loop fusion | flops 991232 | bytes 7938048 | tf_op jit(solution)/shard_map/while/body/eval_jaxpr/jit(_take)/select_n | solution.py:67
  293.6 4.5 %select_n.493 = f32[1024,968]{0,1:T(8,128)} reshape(f32[1024,8,121]{0,2,1:T(8,128)} %broadcast_select_fusion.18) | data formatting | bytes 7929856 | tf_op jit(solution)/shard_map/while/body/eval_jaxpr/jit(_take)/select_n | solution.py:67
  298.1 2.0 constant_dynamic-slice_fusion.20
  300.1 4.6 %convolution_add_fusion.2 = f32[121,1024]{1,0:T(8,128)S(1)} fusion(f32[121,968]{0,1:T(8,128)S(1)} %bitcast.389, f32[1024,968]{0,1:T(8,128)} %select_n.493, f32[121,1024]{1,0:T(8,128)S(1)} %get-tuple-element.159, pred[]{:T(512)S(6)} %compare.29), kind=kOutput, calls=%fused_computation.8.clone.1 | convolution fusion | flops 1439516672 | bytes 5424673 | tf_op jit(solution)/shard_map/while/body/eval_jaxpr/dot_general | solution.py:68
  (133 shorter events, 26.4 us)
Async XLA Ops:
  0.0 95.9 %copy-start = (f32[8,121,121]{2,0,1:T(8,128)S(1)}, f32[8,121,121]{2,0,1:T(8,128)}, u32[]{:S(2)}) copy-start(f32[8,121,121]{2,0,1:T(8,128)} %param.16) | copy-start | bytes 1405540
  0.0 1.5 copy-start.3
  0.0 3.9 %copy-start.14 = (s32[6,256]{1,0:T(8,128)S(1)}, s32[6,256]{1,0:T(8,128)}, u32[]{:S(2)}) copy-start(s32[6,256]{1,0:T(8,128)} %param.13) | copy-start | bytes 18436
  2.0 20.9 %collective-permute-start.6 = (f32[121]{0:T(128)S(1)}, f32[121]{0:T(128)S(1)}, u32[]{:S(2)}, u32[]{:S(2)}) collective-permute-start(f32[121]{0:T(128)S(1)} %convolution_bitcast_fusion.34), channel_id=1, source_target_pairs={{0,1},{1,0},{2,3},{3,2},{4,5},{5,4},{6,7},{7,6},{8,9},{9,8},{10,11... | collective-permute-start | bytes 1460 | tf_op jit(solution)/shard_map/ppermute | solution.py:27
  5.5 91.1 %collective-permute-start = (f32[1,121,256]{1,2,0:T(8,128)}, f32[1,121,256]{1,2,0:T(8,128)}, u32[]{:S(2)}, u32[]{:S(2)}) collective-permute-start(f32[1,121,256]{1,2,0:T(8,128)} %select_bitcast_fusion.5), channel_id=1, source_target_pairs={{0,128},{128,256},{256,384},{1,129},{129,257},{257,385},{2,130},{1... | collective-permute-start | bytes 371720 | tf_op jit(solution)/shard_map/ppermute | solution.py:17
  11.1 90.2 %collective-permute-start.1 = (f32[1,121,256]{1,2,0:T(8,128)}, f32[1,121,256]{1,2,0:T(8,128)}, u32[]{:S(2)}, u32[]{:S(2)}) collective-permute-start(f32[1,121,256]{1,2,0:T(8,128)} %select_bitcast_fusion.4), channel_id=1, source_target_pairs={{128,0},{256,128},{384,256},{129,1},{257,129},{385,257},{130,2},{2... | collective-permute-start | bytes 371720 | tf_op jit(solution)/shard_map/ppermute | solution.py:19
  13.2 7.8 %copy-start.1 = (f32[3,2,121,121]{3,1,2,0:T(2,128)S(1)}, f32[3,2,121,121]{3,1,2,0:T(2,128)}, u32[]{:S(2)}) copy-start(f32[3,2,121,121]{3,1,2,0:T(2,128)} %param.17) | copy-start | bytes 1054156
  13.9 88.3 %collective-permute-start.2 = (f32[1,121,256]{1,2,0:T(8,128)}, f32[1,121,256]{1,2,0:T(8,128)}, u32[]{:S(2)}, u32[]{:S(2)}) collective-permute-start(f32[1,121,256]{1,2,0:T(8,128)} %select_bitcast_fusion.3), channel_id=1, source_target_pairs={{0,32},{32,64},{64,96},{1,33},{33,65},{65,97},{2,34},{34,66},{66,9... | collective-permute-start | bytes 371720 | tf_op jit(solution)/shard_map/ppermute | solution.py:17
  19.5 83.7 %collective-permute-start.3 = (f32[1,121,256]{1,2,0:T(8,128)}, f32[1,121,256]{1,2,0:T(8,128)}, u32[]{:S(2)}, u32[]{:S(2)}) collective-permute-start(f32[1,121,256]{1,2,0:T(8,128)} %select_bitcast_fusion.2), channel_id=1, source_target_pairs={{32,0},{64,32},{96,64},{33,1},{65,33},{97,65},{34,2},{66,34},{98,6... | collective-permute-start | bytes 371720 | tf_op jit(solution)/shard_map/ppermute | solution.py:19
  23.3 5.5 %collective-permute-start.7 = (f32[121]{0:T(128)S(1)}, f32[121]{0:T(128)S(1)}, u32[]{:S(2)}, u32[]{:S(2)}) collective-permute-start(f32[121]{0:T(128)S(1)} %fusion.25), channel_id=1, source_target_pairs={{0,2},{1,3},{2,0},{3,1},{4,6},{5,7},{6,4},{7,5},{8,10},{9,11},{10,... | collective-permute-start | bytes 1460 | tf_op jit(solution)/shard_map/ppermute | solution.py:27
  29.2 6.4 %collective-permute-start.8 = (f32[121]{0:T(128)S(1)}, f32[121]{0:T(128)S(1)}, u32[]{:S(2)}, u32[]{:S(2)}) collective-permute-start(f32[121]{0:T(128)S(1)} %fusion.24), channel_id=1, source_target_pairs={{0,4},{1,5},{2,6},{3,7},{4,0},{5,1},{6,2},{7,3},{8,12},{9,13},{10,... | collective-permute-start | bytes 1460 | tf_op jit(solution)/shard_map/ppermute | solution.py:27
  36.0 9.4 %collective-permute-start.9 = (f32[121]{0:T(128)S(1)}, f32[121]{0:T(128)S(1)}, u32[]{:S(2)}, u32[]{:S(2)}) collective-permute-start(f32[121]{0:T(128)S(1)} %fusion.23), channel_id=1, source_target_pairs={{0,8},{1,9},{2,10},{3,11},{4,12},{5,13},{6,14},{7,15},{8,0},{9,1},... | collective-permute-start | bytes 1460 | tf_op jit(solution)/shard_map/ppermute | solution.py:27
  45.4 33.5 %copy-start.12 = (f32[121]{0:T(128)}, f32[121]{0:T(128)S(1)}, u32[]{:S(2)}) copy-start(f32[121]{0:T(128)S(1)} %collective-permute-done.9) | copy-start | bytes 1456
  45.8 14.2 %collective-permute-start.10 = (f32[121]{0:T(128)S(1)}, f32[121]{0:T(128)S(1)}, u32[]{:S(2)}, u32[]{:S(2)}) collective-permute-start(f32[121]{0:T(128)S(1)} %fusion.22), channel_id=1, source_target_pairs={{0,16},{1,17},{2,18},{3,19},{4,20},{5,21},{6,22},{7,23},{8,24},{9,... | collective-permute-start | bytes 1460 | tf_op jit(solution)/shard_map/ppermute | solution.py:27
  60.3 6.1 %collective-permute-start.11 = (f32[121]{0:T(128)S(1)}, f32[121]{0:T(128)S(1)}, u32[]{:S(2)}, u32[]{:S(2)}) collective-permute-start(f32[121]{0:T(128)S(1)} %fusion.21), channel_id=1, source_target_pairs={{0,32},{1,33},{2,34},{3,35},{4,36},{5,37},{6,38},{7,39},{8,40},{9,... | collective-permute-start | bytes 1460 | tf_op jit(solution)/shard_map/ppermute | solution.py:27
  66.9 7.0 %collective-permute-start.12 = (f32[121]{0:T(128)S(1)}, f32[121]{0:T(128)S(1)}, u32[]{:S(2)}, u32[]{:S(2)}) collective-permute-start(f32[121]{0:T(128)S(1)} %fusion.20), channel_id=1, source_target_pairs={{0,64},{1,65},{2,66},{3,67},{4,68},{5,69},{6,70},{7,71},{8,72},{9,... | collective-permute-start | bytes 1460 | tf_op jit(solution)/shard_map/ppermute | solution.py:27
  74.2 6.1 %collective-permute-start.13 = (f32[121]{0:T(128)S(1)}, f32[121]{0:T(128)S(1)}, u32[]{:S(2)}, u32[]{:S(2)}) collective-permute-start(f32[121]{0:T(128)S(1)} %fusion.19), channel_id=1, source_target_pairs={{0,128},{1,129},{2,130},{3,131},{4,132},{5,133},{6,134},{7,135},{8... | collective-permute-start | bytes 1460 | tf_op jit(solution)/shard_map/ppermute | solution.py:27
  80.7 9.3 %collective-permute-start.14 = (f32[121]{0:T(128)S(1)}, f32[121]{0:T(128)S(1)}, u32[]{:S(2)}, u32[]{:S(2)}) collective-permute-start(f32[121]{0:T(128)S(1)} %fusion.18), channel_id=1, source_target_pairs={{0,256},{1,257},{2,258},{3,259},{4,260},{5,261},{6,262},{7,263},{8... | collective-permute-start | bytes 1460 | tf_op jit(solution)/shard_map/ppermute | solution.py:27
  85.9 6.3 %copy-start.10 = (f32[1,1,121,121]{3,1,2,0:T(1,128)S(1)}, f32[1,1,121,121]{3,1,2,0:T(1,128)}, u32[]{:S(2)}) copy-start(f32[1,1,121,121]{3,1,2,0:T(1,128)} %get-tuple-element.92) | copy-start | bytes 175696
  85.9 6.4 %copy-start.9 = (f32[1,1,121,121]{3,1,2,0:T(1,128)S(1)}, f32[1,1,121,121]{3,1,2,0:T(1,128)}, u32[]{:S(2)}) copy-start(f32[1,1,121,121]{3,1,2,0:T(1,128)} %get-tuple-element.94) | copy-start | bytes 175696
  85.9 6.6 %copy-start.8 = (f32[1,1,121,121]{3,1,2,0:T(1,128)S(1)}, f32[1,1,121,121]{3,1,2,0:T(1,128)}, u32[]{:S(2)}) copy-start(f32[1,1,121,121]{3,1,2,0:T(1,128)} %get-tuple-element.89) | copy-start | bytes 175696
  85.9 6.8 %copy-start.7 = (f32[1,1,121,121]{3,1,2,0:T(1,128)S(1)}, f32[1,1,121,121]{3,1,2,0:T(1,128)}, u32[]{:S(2)}) copy-start(f32[1,1,121,121]{3,1,2,0:T(1,128)} %get-tuple-element.95) | copy-start | bytes 175696
  85.9 7.1 %copy-start.6 = (f32[1,1,121,121]{3,1,2,0:T(1,128)S(1)}, f32[1,1,121,121]{3,1,2,0:T(1,128)}, u32[]{:S(2)}) copy-start(f32[1,1,121,121]{3,1,2,0:T(1,128)} %get-tuple-element.88) | copy-start | bytes 175696
  85.9 7.3 %copy-start.5 = (f32[1,1,121,121]{3,1,2,0:T(1,128)S(1)}, f32[1,1,121,121]{3,1,2,0:T(1,128)}, u32[]{:S(2)}) copy-start(f32[1,1,121,121]{3,1,2,0:T(1,128)} %get-tuple-element.96) | copy-start | bytes 175696
  85.9 7.5 %copy-start.4 = (f32[1,1,121,121]{3,1,2,0:T(1,128)S(1)}, f32[1,1,121,121]{3,1,2,0:T(1,128)}, u32[]{:S(2)}) copy-start(f32[1,1,121,121]{3,1,2,0:T(1,128)} %get-tuple-element.87) | copy-start | bytes 175696
  86.0 8.4 %copy-start.13 = (f32[121]{0:T(128)S(1)}, f32[121]{0:T(128)}, u32[]{:S(2)}) copy-start(f32[121]{0:T(128)} %copy-done.12) | copy-start | bytes 1456
  90.1 6.5 %copy-start.11 = (f32[1,121,256]{1,2,0:T(8,128)S(1)}, f32[1,121,256]{1,2,0:T(8,128)}, u32[]{:S(2)}) copy-start(f32[1,121,256]{1,2,0:T(8,128)} %select_bitcast_fusion) | copy-start | bytes 371716
  90.1 14.1 %collective-permute-start.4 = (f32[1,121,256]{1,2,0:T(8,128)}, f32[1,121,256]{1,2,0:T(8,128)S(1)}, u32[]{:S(2)}, u32[]{:S(2)}) collective-permute-start(f32[1,121,256]{1,2,0:T(8,128)} %select_bitcast_fusion.1), channel_id=1, source_target_pairs={{0,1},{1,2},{2,3},{3,4},{4,5},{5,6},{6,7},{7,8},{8,9},{9,10},{10,1... | collective-permute-start | bytes 371720 | tf_op jit(solution)/shard_map/ppermute | solution.py:17
  94.3 9.8 %copy-start.2 = (s32[32,1024]{1,0:T(8,128)S(1)}, s32[32,1024]{1,0:T(8,128)}, u32[]{:S(2)}) copy-start(s32[32,1024]{1,0:T(8,128)} %param.12) | copy-start | bytes 393220
  96.6 7.6 %collective-permute-start.5 = (f32[1,121,256]{1,2,0:T(8,128)S(1)}, f32[1,121,256]{1,2,0:T(8,128)S(1)}, u32[]{:S(2)}, u32[]{:S(2)}) collective-permute-start(f32[1,121,256]{1,2,0:T(8,128)S(1)} %copy-done.11), channel_id=1, source_target_pairs={{1,0},{2,1},{3,2},{4,3},{5,4},{6,5},{7,6},{8,7},{9,8},{10,9},{11,1... | collective-permute-start | bytes 371720 | tf_op jit(solution)/shard_map/ppermute | solution.py:19
where the time goes:
time: 312 us; the launch traced here: 306 us
  local copies, waits for them, and re-layouts  178 us (57%)
  starting transfers between devices  55.7 us (18%)
  matrix products  26.7 us (9%)
  other arithmetic  25.4 us (8%)
  waiting for transfers between devices  19.2 us (6%)
    gather x8, local copies, waits for them, and re-layouts, add_group(): jnp.take(pool_rows, source_block, axis=0).reshape(per_op, group * num_coef)  133 us
    ppermute x9, starting transfers between devices, from_partner(): lax.ppermute(shard, axis, [(i, i ^ 1 << bit) for i in range(lax.axis_size...  39.2 us
    select_n x8, other arithmetic, add_group(): jnp.take(pool_rows, source_block, axis=0).reshape(per_op, group * num_coef)  20.5 us
    select_n x12, local copies, waits for them, and re-layouts, add_group(): jnp.take(pool_rows, source_block, axis=0).reshape(per_op, group * num_coef)  19.9 us
    ppermute x9, waiting for transfers between devices, from_partner(): lax.ppermute(shard, axis, [(i, i ^ 1 << bit) for i in range(lax.axis_size...  19.2 us
    dot_general x4, matrix products, add_group(): lax.dot_general(ops_block, picked, (((1,), (1,)), ((), ())), precision=HI...  18.4 us
    ppermute x3, starting transfers between devices, extended(): lax.ppermute(tail, axis, [(i, (i + 1) % count) for i in range(ends)])  10.2 us
    dynamic_slice x4, local copies, waits for them, and re-layouts, shards(): lax.scan(add_group, jnp.zeros((num_coef, cells), jnp.float32), (ops_group...  7.91 us
  transfers between devices with their start and end apart: 15, of which 7 were waited for; matrix products, arithmetic and copies ran while one was open for 9% of the time, Pallas kernels for 0%

commit v1 on v0

v1 whole, which is shorter than its diff:
```python
import functools

import jax
import jax.numpy as jnp
from jax import lax
from jax.experimental import pallas as pl
from jax.experimental.pallas import tpu as pltpu
from jax.sharding import PartitionSpec as P

F32, BF16 = jnp.float32, jnp.bfloat16
MESH = pl.DeviceIdType.MESH
NT = (((1,), (1,)), ((), ()))
AXES = ("gx", "gy", "gz")


def split(x):
    hi = x.astype(BF16)
    return hi, (x - hi.astype(F32)).astype(BF16)


def nt(a, b):
    return lax.dot_general(a, b, NT, preferred_element_type=F32)


def dot3(x, wide, narrow):
    hi, lo = split(x)
    return nt(hi, wide) + (nt(lo, wide) + nt(hi, narrow))


def pick8(table, index_of, sub):
    block = None
    for s in range(8):
        row = jnp.broadcast_to(table[pl.ds(index_of(s), 1), :], (8, 128))
        block = row if block is None else jnp.where(sub == s, row, block)
    return block


def kernel(
    sizes, mult, sources, halo, m2l, up, down, side, out,
    cells, own, pool, faces, src_s, halo_s, m2l_v, up_v, down_v, side_v,
    near_w, up_w, down_w, merge_w, cross_w, shift_w, acc,
    mine, line, plane, boxes, sibs, far,
    in_sem, src_sem, face_send, face_recv, line_send, line_recv, plane_send, plane_recv,
):
    coef, ncell, ops, nhalo, ngx, ngy, ngz = sizes
    nplane = ngx * ngy
    gx, gy, gz = (lax.axis_index(a) for a in AXES)
    place = gx * ngy + gy
    me = place * ngz + gz
    zero = lax.shift_right_logical(me, 24)
    offs = tuple(zero + j for j in range(8))
    sub = lax.broadcasted_iota(jnp.int32, (8, 128), 0)

    loads = [
        pltpu.make_async_copy(mult, cells, in_sem.at[0]),
        pltpu.make_async_copy(halo, halo_s, in_sem.at[1]),
        pltpu.make_async_copy(up, up_v, in_sem.at[2]),
        pltpu.make_async_copy(side, side_v, in_sem.at[3]),
        pltpu.make_async_copy(m2l, m2l_v, in_sem.at[4]),
        pltpu.make_async_copy(down, down_v, in_sem.at[5]),
    ]
    for load in loads:
        load.start()

    def source_tile(t):
        g, q = lax.div(t, ncell // 128), lax.rem(t, ncell // 128)
        return pltpu.make_async_copy(
            sources.at[pl.ds(pl.multiple_of(g * 8, 8), 8), pl.ds(pl.multiple_of(q * 128, 128), 128)],
            src_s.at[t],
            src_sem.at[t],
        )

    tiles = ops // 8 * (ncell // 128)

    barrier = pltpu.get_barrier_semaphore()

    def in_line(j):
        return {"gz": lax.rem(gz + j, ngz)}

    def in_plane(j):
        other = lax.rem(place + j, nplane)
        return {"gx": lax.div(other, ngy), "gy": lax.rem(other, ngy)}

    def greet(device_of):
        def one(j, c):
            pl.semaphore_signal(barrier, inc=1, device_id=device_of(j), device_id_type=MESH)
            return c

        return one

    lax.fori_loop(1, ngz, greet(in_line), 0)
    lax.fori_loop(1, nplane, greet(in_plane), 0)

    loads[0].wait()
    for b in range(ncell // 128):
        block = jnp.concatenate(
            [cells[:, b * 128 : (b + 1) * 128], jnp.zeros((128 - coef, 128), F32)], axis=0
        ).T
        own[b * 128 : (b + 1) * 128, :] = block
        pool[b * 128 : (b + 1) * 128, :] = block

    loads[1].wait()
    neighbours = (
        (gx, ngx, lambda i: {"gx": i}),
        (gy, ngy, lambda i: {"gy": i}),
        (gz, ngz, lambda i: {"gz": i}),
    )

    def slot(i):
        return pool.at[pl.ds(ncell + i * nhalo, nhalo)]

    def face_copy(face, land, device):
        return pltpu.make_async_remote_copy(
            src_ref=faces.at[face],
            dst_ref=slot(land),
            send_sem=face_send.at[face],
            recv_sem=face_recv.at[land],
            device_id=device,
            device_id_type=MESH,
        )

    def gather_face(face):
        def part(i, c):
            for r in range(16):
                v = halo_s.at[face, pl.ds(i * 128 + r * 8, 8)]
                faces[face, pl.ds(pl.multiple_of(i * 128 + r * 8, 8), 8), :] = pick8(
                    own, lambda s: v[offs[s]], sub
                )
            return c

        lax.fori_loop(0, nhalo // 128, part, 0)

    gather_face(0)
    gather_face(1)
    pl.semaphore_wait(barrier, ngz - 1 + nplane - 1)
    for a, (at, count, device) in enumerate(neighbours):
        if a:
            gather_face(2 * a)
            gather_face(2 * a + 1)

        @pl.when(at < count - 1)
        def _():
            face_copy(2 * a + 1, 2 * a, device(at + 1)).start()

        @pl.when(at > 0)
        def _():
            face_copy(2 * a, 2 * a + 1, device(at - 1)).start()

        @pl.when(at == 0)
        def _():
            slot(2 * a)[...] = jnp.zeros((nhalo, 128), F32)

        @pl.when(at == count - 1)
        def _():
            slot(2 * a + 1)[...] = jnp.zeros((nhalo, 128), F32)

    def fetch(t, c):
        source_tile(t).start()
        return c

    lax.fori_loop(0, tiles, fetch, 0)

    for w in (up_w, down_w, merge_w, cross_w, shift_w, near_w):
        w[...] = jnp.zeros_like(w)
    loads[2].wait()
    for o in range(8):
        hi, lo = split(up_v[pl.ds(o, coef, 8), :])
        up_w[0, 0:coef, o * 128 : o * 128 + coef] = hi
        up_w[1, 0:coef, o * 128 : o * 128 + coef] = lo

    def add_class(i, total):
        for r in range(16):
            total = total + own[pl.ds(pl.multiple_of(i * 128 + r * 8, 8), 8), :]
        return total

    classes = lax.fori_loop(0, ncell // 128, add_class, jnp.zeros((8, 128), F32))
    flat = jnp.concatenate([classes[o : o + 1, :] for o in range(8)], axis=1)
    box = dot3(jnp.broadcast_to(flat, (8, 1024)), up_w[0], up_w[1])
    mine[0] = box[0:1, :]

    def line_copy(j):
        return pltpu.make_async_remote_copy(
            src_ref=mine.at[0],
            dst_ref=line.at[gz],
            send_sem=line_send.at[j],
            recv_sem=line_recv.at[j],
            device_id=in_line(j),
            device_id_type=MESH,
        )

    def plane_copy(j):
        return pltpu.make_async_remote_copy(
            src_ref=mine.at[1],
            dst_ref=plane.at[place],
            send_sem=plane_send.at[j],
            recv_sem=plane_recv.at[j],
            device_id=in_plane(j),
            device_id_type=MESH,
        )

    def start_all(copy_of):
        def one(j, c):
            copy_of(j).start()
            return c

        return one

    def wait_all(copy_of):
        def one(j, c):
            copy_of(j).wait()
            return c

        return one

    lax.fori_loop(1, ngz, start_all(line_copy), 0)
    line[gz] = box[0:1, :]

    loads[3].wait()
    for b in range(2):
        for a, w in enumerate((merge_w, cross_w, shift_w)):
            hi, lo = split(side_v[a, :, b, :])
            if a == 0:
                w[0, 0:coef, b * 128 : b * 128 + coef] = hi
                w[1, 0:coef, b * 128 : b * 128 + coef] = lo
            else:
                w[b, 0, 0:coef, 0:coef] = hi
                w[b, 1, 0:coef, 0:coef] = lo
    loads[4].wait()

    def split_near(p, c):
        for h in range(2):
            hi, lo = split(m2l_v[pl.ds(p * 2 + h, coef, ops), :])
            near_w[p, 0:coef, h * 128 : h * 128 + coef] = hi
            near_w[p, 128 : 128 + coef, h * 128 : h * 128 + coef] = lo
        return c

    lax.fori_loop(0, ops // 2, split_near, 0)
    loads[5].wait()
    for o in range(8):
        hi, lo = split(down_v[pl.ds(o, coef, 8), :])
        down_w[0, o * 128 : o * 128 + coef, 0:coef] = hi
        down_w[1, o * 128 : o * 128 + coef, 0:coef] = lo
    acc[...] = jnp.zeros_like(acc)
    sibs[...] = jnp.zeros_like(sibs)

    def climb(first, sections, count, index):
        for s in range(sections):
            mask = lax.shift_right_logical(index, s)
            sib = mask + 1 - 2 * lax.rem(mask, 2)
            sibs[first + s : first + s + 1, :] = boxes[pl.ds(sib, 1), :]
            half = count >> (s + 1)
            if half:
                pairs = jnp.concatenate(
                    [boxes[pl.ds(0, half, 2), :], boxes[pl.ds(1, half, 2), :]], axis=1
                )
                boxes[0:half, :] = dot3(pairs, merge_w[0], merge_w[1])

    lax.fori_loop(1, ngz, wait_all(line_copy), 0)
    for i in range(ngz):
        boxes[i : i + 1, :] = line[i]
    line_levels = ngz.bit_length() - 1
    plane_levels = nplane.bit_length() - 1
    climb(0, line_levels, ngz, gz)
    mine[1] = boxes[0:1, :]
    plane[place] = boxes[0:1, :]
    lax.fori_loop(1, nplane, start_all(plane_copy), 0)

    for a, (at, count, device) in enumerate(neighbours):
        @pl.when(at < count - 1)
        def _():
            face_copy(2 * a + 1, 2 * a, device(at + 1)).wait_send()
            face_copy(2 * a, 2 * a + 1, device(at + 1)).wait_recv()

        @pl.when(at > 0)
        def _():
            face_copy(2 * a, 2 * a + 1, device(at - 1)).wait_send()
            face_copy(2 * a + 1, 2 * a, device(at - 1)).wait_recv()

    def arrived(t, c):
        source_tile(t).wait()
        return c

    lax.fori_loop(0, tiles, arrived, 0)

    def near(p, offs):
        def picked(h, n):
            v = src_s.at[lax.div(p, 4) * (ncell // 128) + n // 128, lax.rem(p, 4) * 2 + h, pl.ds(n % 128, 8)]
            return pick8(pool, lambda s: v[offs[s]], sub)

        his, los = [], []
        for n in range(0, ncell, 16):
            rows = [jnp.concatenate([picked(h, n), picked(h, n + 8)], axis=0) for h in range(2)]
            hi, lo = split(jnp.concatenate(rows, axis=1))
            his.append(hi)
            los.append(lo)
        w = near_w[p]
        both = nt(jnp.concatenate(his, axis=0), w)
        low = nt(jnp.concatenate(los, axis=0), w[0:128])
        acc[...] += both[:, 0:128] + both[:, 128:256] + low
        return offs

    lax.fori_loop(0, ops // 2, near, offs)

    lax.fori_loop(1, nplane, wait_all(plane_copy), 0)
    for i in range(nplane):
        boxes[i : i + 1, :] = plane[i]
    climb(line_levels, plane_levels, nplane, place)
    crossed = [dot3(sibs[...], cross_w[b, 0], cross_w[b, 1]) for b in range(2)]
    levels = line_levels + plane_levels
    row = lax.broadcasted_iota(jnp.int32, (16, 128), 0)
    bits = lax.rem(lax.shift_right_logical(jnp.full((16, 128), me, jnp.int32), row), 2)
    far[...] = jnp.where(bits == 0, crossed[0], crossed[1])
    g = jnp.zeros((8, 128), F32)
    for s in reversed(range(levels)):
        b = lax.rem(lax.shift_right_logical(me, s), 2)
        g = dot3(g, shift_w[b, 0], shift_w[b, 1]) + far[s : s + 1, :]
    spread = dot3(g, down_w[0], down_w[1])
    classes = jnp.concatenate([spread[0:1, o * 128 : (o + 1) * 128] for o in range(8)], axis=0)
    tiled = jnp.concatenate([classes] * 16, axis=0)
    for b in range(ncell // 128):
        block = (acc[b * 128 : (b + 1) * 128, :] + tiled).T
        out[:, b * 128 : (b + 1) * 128] = block[0:coef, :]


def shards(mesh, multipoles, sources, halo_cells, m2l_ops, cell_up, cell_down, side_ops):
    coef, ncell = multipoles.shape
    ops = sources.shape[0]
    nhalo = halo_cells.shape[1]
    ngx, ngy, ngz = (mesh.shape[a] for a in AXES)
    nplane = ngx * ngy
    hbm = pl.BlockSpec(memory_space=pl.ANY)
    vmem, dma = pltpu.VMEM, pltpu.SemaphoreType.DMA
    m2l = jnp.transpose(m2l_ops, (1, 0, 2)).reshape(coef * ops, coef)
    up = jnp.transpose(cell_up, (1, 0, 2)).reshape(coef * 8, coef)
    down = jnp.transpose(cell_down, (1, 0, 2)).reshape(coef * 8, coef)
    side = jnp.transpose(side_ops, (0, 2, 1, 3))
    return pl.pallas_call(
        functools.partial(kernel, (coef, ncell, ops, nhalo, ngx, ngy, ngz)),
        out_shape=jax.ShapeDtypeStruct((coef, ncell), F32),
        in_specs=[hbm] * 7,
        out_specs=pl.BlockSpec(memory_space=vmem),
        scratch_shapes=[
            vmem((coef, ncell), F32),
            vmem((ncell, 128), F32),
            vmem((ncell + 6 * nhalo, 128), F32),
            vmem((6, nhalo, 128), F32),
            pltpu.SMEM((ops // 8 * (ncell // 128), 8, 128), jnp.int32),
            pltpu.SMEM((6, nhalo), jnp.int32),
            vmem((coef * ops, coef), F32),
            vmem((coef * 8, coef), F32),
            vmem((coef * 8, coef), F32),
            vmem((3, coef, 2, coef), F32),
            vmem((ops // 2, 256, 256), BF16),
            vmem((2, 128, 1024), BF16),
            vmem((2, 1024, 128), BF16),
            vmem((2, 128, 256), BF16),
            vmem((2, 2, 128, 128), BF16),
            vmem((2, 2, 128, 128), BF16),
            vmem((ncell, 128), F32),
            vmem((2, 1, 128), F32),
            vmem((ngz, 1, 128), F32),
            vmem((nplane, 1, 128), F32),
            vmem((ngz, 128), F32),
            vmem((16, 128), F32),
            vmem((16, 128), F32),
            dma((6,)),
            dma((ops // 8 * (ncell // 128),)),
            dma((6,)),
            dma((6,)),
            dma((ngz,)),
            dma((ngz,)),
            dma((nplane,)),
            dma((nplane,)),
        ],
        compiler_params=pltpu.CompilerParams(
            collective_id=0, has_side_effects=True, vmem_limit_bytes=48 * 2**20
        ),
        cost_estimate=pl.CostEstimate(flops=3 * 10**9, bytes_accessed=4 * 10**6, transcendentals=0),
    )(multipoles, sources, halo_cells, m2l, up, down, side)


def solution(mesh):
    split_cells = P(None, AXES)
    split_rows = P(AXES, None)
    return jax.shard_map(
        functools.partial(shards, mesh),
        mesh=mesh,
        in_specs=(split_cells, split_rows, split_rows, P(), P(), P(), P()),
        out_specs=split_cells,
        check_vma=False,
    )
```

time: 312 us -> 62.6 us (0.20)
  the two profiles are of different devices: /device:TPU:480 before, /device:TPU:1 now
where the time goes in v1:
time: 62.6 us; the launch traced here: 62.2 us
  Pallas kernels  54.1 us (86%)
  local copies, waits for them, and re-layouts  8.04 us (13%)
    pallas_call x1, Pallas kernels, shards(): pl.pallas_call(functools.partial(kernel, (coef, ncell, ops, nhalo, ngx, n...  54.1 us
    unnamed x15, local copies, waits for them, and re-layouts  8.04 us

profile of v1, /device:TPU:1, one launch (start us, length us, event | category | flops | bytes accessed | tf_op | source)
XLA Modules:
  0.0 62.2 jit_solution(6501228743637599655)
XLA Ops:
  0.0 0.0 copy-start
  0.0 1.5 %copy-done = f32[32,121,121]{2,0,1:T(8,128)S(1)} copy-done((f32[32,121,121]{2,0,1:T(8,128)S(1)}, f32[32,121,121]{2,0,1:T(8,128)}, u32[]{:S(2)}) %copy-start) | copy-done | bytes 1874072
  1.6 0.0 copy-start.1
  1.6 1.0 %copy-done.1 = f32[121,1024]{1,0:T(8,128)S(1)} copy-done((f32[121,1024]{1,0:T(8,128)S(1)}, f32[121,1024]{1,0:T(8,128)}, u32[]{:S(2)}) %copy-start.1) | copy-done | bytes 495640
  2.6 0.0 copy-start.2
  2.6 1.0 %copy-done.2 = f32[8,121,121]{2,0,1:T(8,128)S(1)} copy-done((f32[8,121,121]{2,0,1:T(8,128)S(1)}, f32[8,121,121]{2,0,1:T(8,128)}, u32[]{:S(2)}) %copy-start.2) | copy-done | bytes 468536
  3.6 0.0 copy-start.3
  3.6 1.0 %copy-done.3 = f32[8,121,121]{2,0,1:T(8,128)S(1)} copy-done((f32[8,121,121]{2,0,1:T(8,128)S(1)}, f32[8,121,121]{2,0,1:T(8,128)}, u32[]{:S(2)}) %copy-start.3) | copy-done | bytes 468536
  4.7 0.0 copy-start.4
  4.7 1.0 %copy-done.4 = f32[3,2,121,121]{3,1,2,0:T(2,128)S(1)} copy-done((f32[3,2,121,121]{3,1,2,0:T(2,128)S(1)}, f32[3,2,121,121]{3,1,2,0:T(2,128)}, u32[]{:S(2)}) %copy-start.4) | copy-done | bytes 351408
  5.6 0.0 copy-start.5
  5.6 0.9 %copy-done.5 = s32[32,1024]{1,0:T(8,128)S(1)} copy-done((s32[32,1024]{1,0:T(8,128)S(1)}, s32[32,1024]{1,0:T(8,128)}, u32[]{:S(2)}) %copy-start.5) | copy-done | bytes 131096
  6.6 0.0 copy-start.6
  6.6 0.7 %copy-done.6 = s32[6,256]{1,0:T(8,128)S(1)} copy-done((s32[6,256]{1,0:T(8,128)S(1)}, s32[6,256]{1,0:T(8,128)}, u32[]{:S(2)}) %copy-start.6) | copy-done | bytes 6168
  7.2 54.1 %shard_map.73 = f32[121,1024]{1,0:T(8,128)S(1)} custom-call(f32[121,1024]{1,0:T(8,128)S(1)} %copy-done.1, s32[32,1024]{1,0:T(8,128)S(1)} %copy-done.5, s32[6,256]{1,0:T(8,128)S(1)} %copy-done.6, f32[3872,121]{1,0:T(8,128)S(1)} %bitcast.10, f32[968,121]{1,0:T(8,128)S(1)} %bitcast.11, f32[968,121]{1,0:T(8,128)S(1)} %bitcast.12, f32[3,121,2,121]{3,2,1,0:T(2,128)S(1)} %bitcast.13), custom_call_target="tpu_custom_call" | custom-call | flops 3000000000 | bytes 4000000 | tf_op jit(solution)/shard_map/pallas_call | solution.py:337
  61.4 0.8 %copy.9 = f32[121,1024]{1,0:T(8,128)} copy(f32[121,1024]{1,0:T(8,128)S(1)} %shard_map.73) | data formatting | bytes 991232
Async XLA Ops:
  0.0 1.6 %copy-start = (f32[32,121,121]{2,0,1:T(8,128)S(1)}, f32[32,121,121]{2,0,1:T(8,128)}, u32[]{:S(2)}) copy-start(f32[32,121,121]{2,0,1:T(8,128)} %param.10) | copy-start | bytes 5622148
  1.6 1.0 %copy-start.1 = (f32[121,1024]{1,0:T(8,128)S(1)}, f32[121,1024]{1,0:T(8,128)}, u32[]{:S(2)}) copy-start(f32[121,1024]{1,0:T(8,128)} %mult.1) | copy-start | bytes 1486852
  2.6 1.0 %copy-start.2 = (f32[8,121,121]{2,0,1:T(8,128)S(1)}, f32[8,121,121]{2,0,1:T(8,128)}, u32[]{:S(2)}) copy-start(f32[8,121,121]{2,0,1:T(8,128)} %param.11) | copy-start | bytes 1405540
  3.6 1.0 %copy-start.3 = (f32[8,121,121]{2,0,1:T(8,128)S(1)}, f32[8,121,121]{2,0,1:T(8,128)}, u32[]{:S(2)}) copy-start(f32[8,121,121]{2,0,1:T(8,128)} %param.12) | copy-start | bytes 1405540
  4.7 1.0 %copy-start.4 = (f32[3,2,121,121]{3,1,2,0:T(2,128)S(1)}, f32[3,2,121,121]{3,1,2,0:T(2,128)}, u32[]{:S(2)}) copy-start(f32[3,2,121,121]{3,1,2,0:T(2,128)} %param.13) | copy-start | bytes 1054156
  5.6 0.9 %copy-start.5 = (s32[32,1024]{1,0:T(8,128)S(1)}, s32[32,1024]{1,0:T(8,128)}, u32[]{:S(2)}) copy-start(s32[32,1024]{1,0:T(8,128)} %sources.1) | copy-start | bytes 393220
  6.6 0.7 %copy-start.6 = (s32[6,256]{1,0:T(8,128)S(1)}, s32[6,256]{1,0:T(8,128)}, u32[]{:S(2)}) copy-start(s32[6,256]{1,0:T(8,128)} %halo.1) | copy-start | bytes 18436

commit v2 on v1

--- a/solution.py
+++ b/solution.py
@@ -11,6 +11,8 @@
 MESH = pl.DeviceIdType.MESH
 NT = (((1,), (1,)), ((), ()))
 AXES = ("gx", "gy", "gz")
+REACH = 4
+LINE_STEP = 12
 
 
 def split(x):
@@ -40,7 +42,7 @@
     cells, own, pool, faces, src_s, halo_s, m2l_v, up_v, down_v, side_v,
     near_w, up_w, down_w, merge_w, cross_w, shift_w, acc,
     mine, line, plane, boxes, sibs, far,
-    in_sem, src_sem, face_send, face_recv, line_send, line_recv, plane_send, plane_recv,
+    in_sem, src_sem, known, face_send, face_recv, line_send, line_recv, plane_send, plane_recv,
 ):
     coef, ncell, ops, nhalo, ngx, ngy, ngz = sizes
     nplane = ngx * ngy
@@ -59,8 +61,8 @@
         pltpu.make_async_copy(m2l, m2l_v, in_sem.at[4]),
         pltpu.make_async_copy(down, down_v, in_sem.at[5]),
     ]
-    for load in loads:
-        load.start()
+    loads[0].start()
+    loads[1].start()
 
     def source_tile(t):
         g, q = lax.div(t, ncell // 128), lax.rem(t, ncell // 128)
@@ -81,15 +83,34 @@
         other = lax.rem(place + j, nplane)
         return {"gx": lax.div(other, ngy), "gy": lax.rem(other, ngy)}
 
-    def greet(device_of):
-        def one(j, c):
-            pl.semaphore_signal(barrier, inc=1, device_id=device_of(j), device_id_type=MESH)
-            return c
-
-        return one
-
-    lax.fori_loop(1, ngz, greet(in_line), 0)
-    lax.fori_loop(1, nplane, greet(in_plane), 0)
+    def tell(semaphore, apart):
+        @pl.when(gz + apart < ngz)
+        def _():
+            pl.semaphore_signal(semaphore, inc=1, device_id={"gz": gz + apart}, device_id_type=MESH)
+
+        @pl.when(gz >= apart)
+        def _():
+            pl.semaphore_signal(semaphore, inc=1, device_id={"gz": gz - apart}, device_id_type=MESH)
+
+    def greet(j, c):
+        pl.semaphore_signal(barrier, inc=1, device_id=in_plane(j), device_id_type=MESH)
+        return c
+
+    for j in range(1, REACH + 1):
+        tell(barrier, j)
+    lax.fori_loop(1, nplane, greet, 0)
+    greeted = jnp.minimum(gz, REACH) + jnp.minimum(ngz - 1 - gz, REACH) + nplane - 1
+
+    rounds = max(0, (ngz // REACH).bit_length() - 1)
+
+    def call(r):
+        tell(known.at[r], REACH << r)
+
+    def hear(r):
+        apart = REACH << r
+        pl.semaphore_wait(
+            known.at[r], (gz >= apart).astype(jnp.int32) + (gz + apart < ngz).astype(jnp.int32)
+        )
 
     loads[0].wait()
     for b in range(ncell // 128):
@@ -99,6 +120,8 @@
         own[b * 128 : (b + 1) * 128, :] = block
         pool[b * 128 : (b + 1) * 128, :] = block
 
+    for load in loads[2:]:
+        load.start()
     loads[1].wait()
     neighbours = (
         (gx, ngx, lambda i: {"gx": i}),
@@ -130,14 +153,10 @@
 
         lax.fori_loop(0, nhalo // 128, part, 0)
 
-    gather_face(0)
-    gather_face(1)
-    pl.semaphore_wait(barrier, ngz - 1 + nplane - 1)
+    for face in range(6):
+        gather_face(face)
+    pl.semaphore_wait(barrier, greeted)
     for a, (at, count, device) in enumerate(neighbours):
-        if a:
-            gather_face(2 * a)
-            gather_face(2 * a + 1)
-
         @pl.when(at < count - 1)
         def _():
             face_copy(2 * a + 1, 2 * a, device(at + 1)).start()
@@ -146,19 +165,22 @@
         def _():
             face_copy(2 * a, 2 * a + 1, device(at - 1)).start()
 
-        @pl.when(at == 0)
-        def _():
-            slot(2 * a)[...] = jnp.zeros((nhalo, 128), F32)
-
-        @pl.when(at == count - 1)
-        def _():
-            slot(2 * a + 1)[...] = jnp.zeros((nhalo, 128), F32)
+    call(0)
 
     def fetch(t, c):
         source_tile(t).start()
         return c
 
     lax.fori_loop(0, tiles, fetch, 0)
+
+    for a, (at, count, _) in enumerate(neighbours):
+        @pl.when(at == 0)
+        def _():
+            slot(2 * a)[...] = jnp.zeros((nhalo, 128), F32)
+
+        @pl.when(at == count - 1)
+        def _():
+            slot(2 * a + 1)[...] = jnp.zeros((nhalo, 128), F32)
 
     for w in (up_w, down_w, merge_w, cross_w, shift_w, near_w):
         w[...] = jnp.zeros_like(w)
@@ -177,43 +199,6 @@
     flat = jnp.concatenate([classes[o : o + 1, :] for o in range(8)], axis=1)
     box = dot3(jnp.broadcast_to(flat, (8, 1024)), up_w[0], up_w[1])
     mine[0] = box[0:1, :]
-
-    def line_copy(j):
-        return pltpu.make_async_remote_copy(
-            src_ref=mine.at[0],
-            dst_ref=line.at[gz],
-            send_sem=line_send.at[j],
-            recv_sem=line_recv.at[j],
-            device_id=in_line(j),
-            device_id_type=MESH,
-        )
-
-    def plane_copy(j):
-        return pltpu.make_async_remote_copy(
-            src_ref=mine.at[1],
-            dst_ref=plane.at[place],
-            send_sem=plane_send.at[j],
-            recv_sem=plane_recv.at[j],
-            device_id=in_plane(j),
-            device_id_type=MESH,
-        )
-
-    def start_all(copy_of):
-        def one(j, c):
-            copy_of(j).start()
-            return c
-
-        return one
-
-    def wait_all(copy_of):
-        def one(j, c):
-            copy_of(j).wait()
-            return c
-
-        return one
-
-    lax.fori_loop(1, ngz, start_all(line_copy), 0)
-    line[gz] = box[0:1, :]
 
     loads[3].wait()
     for b in range(2):
@@ -243,6 +228,42 @@
     acc[...] = jnp.zeros_like(acc)
     sibs[...] = jnp.zeros_like(sibs)
 
+    def line_copy(j):
+        return pltpu.make_async_remote_copy(
+            src_ref=mine.at[0],
+            dst_ref=line.at[gz],
+            send_sem=line_send.at[j],
+            recv_sem=line_recv.at[j],
+            device_id=in_line(j),
+            device_id_type=MESH,
+        )
+
+    def plane_copy(j):
+        return pltpu.make_async_remote_copy(
+            src_ref=mine.at[1],
+            dst_ref=plane.at[place],
+            send_sem=plane_send.at[j],
+            recv_sem=plane_recv.at[j],
+            device_id=in_plane(j),
+            device_id_type=MESH,
+        )
+
+    def start_all(copy_of):
+        def one(j, c):
+            copy_of(j).start()
+            return c
+
+        return one
+
+    def wait_all(copy_of):
+        def one(j, c):
+            copy_of(j).wait()
+            return c
+
+        return one
+
+    line[gz] = box[0:1, :]
+
     def climb(first, sections, count, index):
         for s in range(sections):
             mask = lax.shift_right_logical(index, s)
@@ -255,15 +276,17 @@
                 )
                 boxes[0:half, :] = dot3(pairs, merge_w[0], merge_w[1])
 
-    lax.fori_loop(1, ngz, wait_all(line_copy), 0)
-    for i in range(ngz):
-        boxes[i : i + 1, :] = line[i]
     line_levels = ngz.bit_length() - 1
     plane_levels = nplane.bit_length() - 1
-    climb(0, line_levels, ngz, gz)
-    mine[1] = boxes[0:1, :]
-    plane[place] = boxes[0:1, :]
-    lax.fori_loop(1, nplane, start_all(plane_copy), 0)
+
+    def line_done():
+        lax.fori_loop(1, ngz, wait_all(line_copy), 0)
+        for i in range(ngz):
+            boxes[i : i + 1, :] = line[i]
+        climb(0, line_levels, ngz, gz)
+        mine[1] = boxes[0:1, :]
+        plane[place] = boxes[0:1, :]
+        lax.fori_loop(1, nplane, start_all(plane_copy), 0)
 
     for a, (at, count, device) in enumerate(neighbours):
         @pl.when(at < count - 1)
@@ -282,7 +305,26 @@
 
     lax.fori_loop(0, tiles, arrived, 0)
 
+    lead = jnp.maximum(ngz // 2 - gz, 0)
+
     def near(p, offs):
+        @pl.when(p == 0)
+        def _():
+            hear(0)
+            call(1)
+
+        @pl.when(p == 1 + lax.div(jnp.minimum(lead, 12) * 5, 12))
+        def _():
+            hear(1)
+            call(2)
+
+        @pl.when(p == 2 + lax.div(lead, 2))
+        def _():
+            hear(2)
+            lax.fori_loop(1, ngz, start_all(line_copy), 0)
+
+        pl.when(p == LINE_STEP)(line_done)
+
         def picked(h, n):
             v = src_s.at[lax.div(p, 4) * (ncell // 128) + n // 128, lax.rem(p, 4) * 2 + h, pl.ds(n % 128, 8)]
             return pick8(pool, lambda s: v[offs[s]], sub)
@@ -316,9 +358,9 @@
         g = dot3(g, shift_w[b, 0], shift_w[b, 1]) + far[s : s + 1, :]
     spread = dot3(g, down_w[0], down_w[1])
     classes = jnp.concatenate([spread[0:1, o * 128 : (o + 1) * 128] for o in range(8)], axis=0)
-    tiled = jnp.concatenate([classes] * 16, axis=0)
+    spread = jnp.concatenate([classes] * 16, axis=0).T
     for b in range(ncell // 128):
-        block = (acc[b * 128 : (b + 1) * 128, :] + tiled).T
+        block = acc[b * 128 : (b + 1) * 128, :].T + spread
         out[:, b * 128 : (b + 1) * 128] = block[0:coef, :]
 
 
@@ -328,7 +370,7 @@
     nhalo = halo_cells.shape[1]
     ngx, ngy, ngz = (mesh.shape[a] for a in AXES)
     nplane = ngx * ngy
-    hbm = pl.BlockSpec(memory_space=pl.ANY)
+    hbm = pl.BlockSpec(memory_space=pltpu.HBM)
     vmem, dma = pltpu.VMEM, pltpu.SemaphoreType.DMA
     m2l = jnp.transpose(m2l_ops, (1, 0, 2)).reshape(coef * ops, coef)
     up = jnp.transpose(cell_up, (1, 0, 2)).reshape(coef * 8, coef)
@@ -365,6 +407,7 @@
             vmem((16, 128), F32),
             dma((6,)),
             dma((ops // 8 * (ncell // 128),)),
+            pltpu.SemaphoreType.REGULAR((4,)),
             dma((6,)),
             dma((6,)),
             dma((ngz,)),
@@ -373,7 +416,7 @@
             dma((nplane,)),
         ],
         compiler_params=pltpu.CompilerParams(
-            collective_id=0, has_side_effects=True, vmem_limit_bytes=48 * 2**20
+            collective_id=0, has_side_effects=True, vmem_limit_bytes=63 * 2**20
         ),
         cost_estimate=pl.CostEstimate(flops=3 * 10**9, bytes_accessed=4 * 10**6, transcendentals=0),
     )(multipoles, sources, halo_cells, m2l, up, down, side)

time: 62.6 us -> 48.4 us (0.77)
  the two profiles are of different devices: /device:TPU:1 before, /device:TPU:480 now
where the time goes in v2:
time: 48.4 us; the launch traced here: 47.6 us
  Pallas kernels  45.7 us (94%)
  local copies, waits for them, and re-layouts  1.89 us (4%)
    pallas_call x1, Pallas kernels, shards(): pl.pallas_call(functools.partial(kernel, (coef, ncell, ops, nhalo, ngx, n...  45.7 us
    unnamed x1, local copies, waits for them, and re-layouts  1.89 us

profile of v2, /device:TPU:480, one launch (start us, length us, event | category | flops | bytes accessed | tf_op | source)
XLA Modules:
  0.0 47.6 jit_solution(4272402621949290015)
XLA Ops:
  0.0 45.7 %shard_map.73 = f32[121,1024]{1,0:T(8,128)} custom-call(f32[121,1024]{1,0:T(8,128)} %mult.1, s32[32,1024]{1,0:T(8,128)} %sources.1, s32[6,256]{1,0:T(8,128)} %halo.1, f32[3872,121]{1,0:T(8,128)} %bitcast.10, f32[968,121]{1,0:T(8,128)} %bitcast.11, f32[968,121]{1,0:T(8,128)} %bitcast.12, f32[3,121,2,121]{3,2,1,0:T(2,128)} %bitcast.13), custom_call_target="tpu_custom_call" | custom-call | flops 3000000000 | bytes 4000000 | tf_op jit(solution)/shard_map/pallas_call | solution.py:379
  45.7 1.9 %copy.9 = f32[121,1024]{1,0:T(8,128)} copy(f32[121,1024]{1,0:T(8,128)} %shard_map.73) | data formatting | bytes 991232

commit v3 on v2

v3 whole, which is shorter than its diff:
```python
import functools

import jax
import jax.numpy as jnp
from jax import lax
from jax.experimental import pallas as pl
from jax.experimental.pallas import tpu as pltpu
from jax.sharding import PartitionSpec as P

F32, BF16 = jnp.float32, jnp.bfloat16
MESH = pl.DeviceIdType.MESH
NT = (((1,), (1,)), ((), ()))
AXES = ("gx", "gy", "gz")
UP_STEP = 9
LINE_STEP = 12


def split(x):
    hi = x.astype(BF16)
    return hi, (x - hi.astype(F32)).astype(BF16)


def nt(a, b):
    return lax.dot_general(a, b, NT, preferred_element_type=F32)


def dot3(x, wide, narrow):
    hi, lo = split(x)
    return nt(hi, wide) + (nt(lo, wide) + nt(hi, narrow))


def nn3(a, b):
    ah, al = split(a)
    bh, bl = split(b)
    dot = functools.partial(jnp.dot, preferred_element_type=F32)
    return dot(ah, bh) + (dot(al, bh) + dot(ah, bl))


def pick8(table, index_of, sub):
    block = None
    for s in range(8):
        row = jnp.broadcast_to(table[pl.ds(index_of(s), 1), :], (8, 128))
        block = row if block is None else jnp.where(sub == s, row, block)
    return block


def kernel(
    sizes, mult, sources, halo, m2l, up, down, side, out,
    cells, own, pool, faces, src_s, halo_s, m2l_v, up_v, down_v, side_v,
    near_w, up_w, down_w, side_w, merge_w, merge4_w, far_w, acc,
    mine, line, plane, boxes, sibs,
    in_sem, src_sem, face_send, face_recv, line_send, line_recv, plane_send, plane_recv,
):
    coef, ncell, ops, nhalo, ngx, ngy, ngz = sizes
    nplane = ngx * ngy
    gx, gy, gz = (lax.axis_index(a) for a in AXES)
    place = gx * ngy + gy
    me = place * ngz + gz
    zero = lax.shift_right_logical(me, 24)
    offs = tuple(zero + j for j in range(8))
    sub = lax.broadcasted_iota(jnp.int32, (8, 128), 0)

    loads = [
        pltpu.make_async_copy(mult, cells, in_sem.at[0]),
        pltpu.make_async_copy(halo, halo_s, in_sem.at[1]),
        pltpu.make_async_copy(up, up_v, in_sem.at[2]),
        pltpu.make_async_copy(side, side_v, in_sem.at[3]),
        pltpu.make_async_copy(m2l, m2l_v, in_sem.at[4]),
        pltpu.make_async_copy(down, down_v, in_sem.at[5]),
    ]
    loads[0].start()
    loads[1].start()

    def source_tile(t):
        g, q = lax.div(t, ncell // 128), lax.rem(t, ncell // 128)
        return pltpu.make_async_copy(
            sources.at[pl.ds(pl.multiple_of(g * 8, 8), 8), pl.ds(pl.multiple_of(q * 128, 128), 128)],
            src_s.at[t],
            src_sem.at[0],
        )

    tiles = ops // 8 * (ncell // 128)

    barrier = pltpu.get_barrier_semaphore()

    def in_plane(j):
        other = lax.rem(place + j, nplane)
        return {"gx": lax.div(other, ngy), "gy": lax.rem(other, ngy)}

    def greet(device):
        pl.semaphore_signal(barrier, inc=1, device_id=device, device_id_type=MESH)

    def greet_plane(j, c):
        greet(in_plane(j))
        return c

    def greet_up(i, c):
        greet({"gz": i})
        return c

    pl.when(gz > 0)(lambda: greet({"gz": gz - 1}))
    lax.fori_loop(gz + 1, ngz, greet_up, 0)
    lax.fori_loop(1, nplane, greet_plane, 0)
    greeted = nplane - 1 + gz + (gz < ngz - 1).astype(jnp.int32)

    loads[0].wait()
    for b in range(ncell // 128):
        block = jnp.concatenate(
            [cells[:, b * 128 : (b + 1) * 128], jnp.zeros((128 - coef, 128), F32)], axis=0
        ).T
        own[b * 128 : (b + 1) * 128, :] = block
        pool[b * 128 : (b + 1) * 128, :] = block

    for load in loads[2:]:
        load.start()
    loads[1].wait()
    neighbours = (
        (gx, ngx, lambda i: {"gx": i}),
        (gy, ngy, lambda i: {"gy": i}),
        (gz, ngz, lambda i: {"gz": i}),
    )

    def slot(i):
        return pool.at[pl.ds(ncell + i * nhalo, nhalo)]

    def face_copy(face, land, device):
        return pltpu.make_async_remote_copy(
            src_ref=faces.at[face],
            dst_ref=slot(land),
            send_sem=face_send.at[face],
            recv_sem=face_recv.at[land],
            device_id=device,
            device_id_type=MESH,
        )

    def gather_face(face):
        def part(i, c):
            for r in range(16):
                v = halo_s.at[face, pl.ds(i * 128 + r * 8, 8)]
                faces[face, pl.ds(pl.multiple_of(i * 128 + r * 8, 8), 8), :] = pick8(
                    own, lambda s: v[offs[s]], sub
                )
            return c

        lax.fori_loop(0, nhalo // 128, part, 0)

    for a, (at, count, device) in enumerate(neighbours):
        gather_face(2 * a)
        gather_face(2 * a + 1)
        if a == 0:
            pl.semaphore_wait(barrier, greeted)

        @pl.when(at < count - 1)
        def _():
            face_copy(2 * a + 1, 2 * a, device(at + 1)).start()

        @pl.when(at > 0)
        def _():
            face_copy(2 * a, 2 * a + 1, device(at - 1)).start()

    def fetch(t, c):
        source_tile(t).start()
        return c

    lax.fori_loop(0, tiles, fetch, 0)

    for a, (at, count, _) in enumerate(neighbours):
        @pl.when(at == 0)
        def _():
            slot(2 * a)[...] = jnp.zeros((nhalo, 128), F32)

        @pl.when(at == count - 1)
        def _():
            slot(2 * a + 1)[...] = jnp.zeros((nhalo, 128), F32)

    for w in (up_w, down_w, side_w, near_w):
        w[...] = jnp.zeros_like(w)
    loads[2].wait()
    for o in range(8):
        hi, lo = split(up_v[pl.ds(o, coef, 8), :])
        up_w[0, 0:coef, o * 128 : o * 128 + coef] = hi
        up_w[1, 0:coef, o * 128 : o * 128 + coef] = lo

    def add_class(i, total):
        for r in range(16):
            total = total + own[pl.ds(pl.multiple_of(i * 128 + r * 8, 8), 8), :]
        return total

    classes = lax.fori_loop(0, ncell // 128, add_class, jnp.zeros((8, 128), F32))
    flat = jnp.concatenate([classes[o : o + 1, :] for o in range(8)], axis=1)
    box = dot3(jnp.broadcast_to(flat, (8, 1024)), up_w[0], up_w[1])
    mine[0] = box[0:1, :]

    loads[3].wait()
    for a in range(3):
        for b in range(2):
            side_w[a, b, 0:coef, 0:coef] = side_v[a, :, b, :]
    merge = jnp.concatenate([side_w[0, 0], side_w[0, 1]], axis=1)
    merge_w[0], merge_w[1] = split(merge)
    four = nn3(jnp.concatenate([side_w[0, 0], side_w[0, 1]], axis=0), merge)
    merge4_w[0], merge4_w[1] = split(jnp.concatenate([four[0:128], four[128:256]], axis=1))
    levels = (ngz * nplane).bit_length() - 1
    turn = [lax.rem(lax.shift_right_logical(me, s), 2) for s in range(levels)]
    step = [side_w[2, turn[s]] for s in range(levels)]
    two = [nn3(step[s], step[s + 1]) for s in range(0, levels - 1, 2)]
    third = nn3(two[0], jnp.concatenate([step[2], two[1]], axis=1))
    rest = nn3(two[2], jnp.concatenate([step[6], two[3]], axis=1))
    upper = nn3(third[:, 128:256], jnp.concatenate([step[4], two[2], rest], axis=1))
    way = [None, step[0], two[0], third[:, 0:128], third[:, 128:256]]
    way += [upper[:, i * 128 : (i + 1) * 128] for i in range(4)]
    for s in range(levels):
        cross = side_w[1, turn[s]]
        far_w[0, :, s * 128 : (s + 1) * 128], far_w[1, :, s * 128 : (s + 1) * 128] = split(
            nn3(way[s], cross) if s else cross
        )
    loads[5].wait()
    for o in range(8):
        hi, lo = split(down_v[pl.ds(o, coef, 8), :])
        down_w[0, o * 128 : o * 128 + coef, 0:coef] = hi
        down_w[1, o * 128 : o * 128 + coef, 0:coef] = lo
    acc[...] = jnp.zeros_like(acc)
    sibs[...] = jnp.zeros_like(sibs)

    def line_copy(sender, device):
        return pltpu.make_async_remote_copy(
            src_ref=mine.at[0],
            dst_ref=line.at[sender],
            send_sem=line_send.at[0],
            recv_sem=line_recv.at[sender],
            device_id={"gz": device},
            device_id_type=MESH,
        )

    def send_box(to, c):
        line_copy(gz, to).start()
        return c

    def get_box(sender, c):
        line_copy(sender, sender).wait_recv()
        return c

    def plane_copy(j):
        return pltpu.make_async_remote_copy(
            src_ref=mine.at[1],
            dst_ref=plane.at[place],
            send_sem=plane_send.at[0],
            recv_sem=plane_recv.at[0],
            device_id=in_plane(j),
            device_id_type=MESH,
        )

    def send_top(j, c):
        plane_copy(j).start()
        return c

    def all_of(buffer, count, send, recv):
        every = buffer.at[pl.ds(0, count - 1)]
        return pltpu.make_async_remote_copy(
            src_ref=every,
            dst_ref=every,
            send_sem=send.at[0],
            recv_sem=recv.at[0],
            device_id=in_plane(1),
            device_id_type=MESH,
        )

    lax.fori_loop(0, gz, send_box, 0)
    line[gz] = box[0:1, :]

    def quads(count):
        rows = [boxes[pl.ds(i, count // 4, 4), :] for i in range(4)]
        return dot3(jnp.concatenate(rows, axis=1), merge4_w[0], merge4_w[1])

    def pair(index):
        return jnp.concatenate([boxes[pl.ds(2 * index, 1), :], boxes[pl.ds(2 * index + 1, 1), :]], axis=1)

    def merged(rows):
        return dot3(jnp.concatenate(rows, axis=0), merge_w[0], merge_w[1])

    def sibling(index, s):
        mask = lax.shift_right_logical(index, s)
        return mask + 1 - 2 * lax.rem(mask, 2)

    def line_done():
        lax.fori_loop(0, gz, get_box, 0)
        for i in range(ngz):
            boxes[i : i + 1, :] = line[i]
        sibs[0:1, :] = boxes[pl.ds(sibling(gz, 0), 1), :]
        first = pair(sibling(gz, 1))
        boxes[0:8, :] = quads(32)
        sibs[2:3, :] = boxes[pl.ds(sibling(gz, 2), 1), :]
        third = pair(sibling(gz, 3))
        boxes[0:2, :] = quads(8)
        sibs[4:5, :] = boxes[pl.ds(sibling(gz, 4), 1), :]
        top = merged([first, third, pair(0)])
        sibs[1:2, :] = top[0:1, :]
        sibs[3:4, :] = top[1:2, :]
        mine[1] = top[2:3, :]
        plane[place] = top[2:3, :]
        lax.fori_loop(1, nplane, send_top, 0)

    for a, (at, count, device) in enumerate(neighbours):
        @pl.when(at < count - 1)
        def _():
            face_copy(2 * a + 1, 2 * a, device(at + 1)).wait_send()
            face_copy(2 * a, 2 * a + 1, device(at + 1)).wait_recv()

        @pl.when(at > 0)
        def _():
            face_copy(2 * a, 2 * a + 1, device(at - 1)).wait_send()
            face_copy(2 * a + 1, 2 * a, device(at - 1)).wait_recv()

    pltpu.make_async_copy(src_s, src_s, src_sem.at[0]).wait()

    def split_near(p, to):
        for h in range(2):
            hi, lo = split(m2l_v[pl.ds(p * 2 + h, coef, ops), :])
            near_w[to, 0:coef, h * 128 : h * 128 + coef] = hi
            near_w[to, 128 : 128 + coef, h * 128 : h * 128 + coef] = lo

    loads[4].wait()
    split_near(0, 0)

    def near(p, offs):
        @pl.when(p == UP_STEP)
        def _():
            lax.fori_loop(gz + 1, ngz, get_box, 0)
            lax.fori_loop(gz + 1, ngz, send_box, 0)

        pl.when(p == LINE_STEP)(line_done)

        def picked(h, n):
            v = src_s.at[lax.div(p, 4) * (ncell // 128) + n // 128, lax.rem(p, 4) * 2 + h, pl.ds(n % 128, 8)]
            return pick8(pool, lambda s: v[offs[s]], sub)

        now = lax.rem(p, 2)
        his, los = [], []
        for n in range(0, ncell, 16):
            rows = [jnp.concatenate([picked(h, n), picked(h, n + 8)], axis=0) for h in range(2)]
            hi, lo = split(jnp.concatenate(rows, axis=1))
            his.append(hi)
            los.append(lo)
        w = near_w[now]
        both = nt(jnp.concatenate(his, axis=0), w)
        low = nt(jnp.concatenate(los, axis=0), w[0:128])
        acc[...] += both[:, 0:128] + both[:, 128:256] + low
        split_near(jnp.minimum(p + 1, ops // 2 - 1), 1 - now)
        return offs

    lax.fori_loop(0, ops // 2, near, offs)

    all_of(plane, nplane, plane_send, plane_recv).wait()
    all_of(line, ngz, line_send, line_recv).wait_send()
    for i in range(nplane):
        boxes[i : i + 1, :] = plane[i]
    known_sibs = [sibs[s : s + 1, :] for s in range(5)]
    known_sibs.append(boxes[pl.ds(sibling(place, 0), 1), :])
    sixth = pair(sibling(place, 1))
    boxes[0:4, :] = quads(16)
    known_sibs.append(None)
    known_sibs.append(boxes[pl.ds(sibling(place, 2), 1), :])
    last = merged([sixth, pair(sibling(place, 3))])
    known_sibs[6] = last[0:1, :]
    known_sibs.append(last[1:2, :])
    every = jnp.concatenate(known_sibs, axis=1)
    g = dot3(every, far_w[0, :, 0 : levels * 128], far_w[1, :, 0 : levels * 128])
    spread = dot3(g, down_w[0], down_w[1])
    classes = jnp.concatenate([spread[0:1, o * 128 : (o + 1) * 128] for o in range(8)], axis=0)
    spread = jnp.concatenate([classes] * 16, axis=0).T
    for b in range(ncell // 128):
        block = acc[b * 128 : (b + 1) * 128, :].T + spread
        out[:, b * 128 : (b + 1) * 128] = block[0:coef, :]


def shards(mesh, multipoles, sources, halo_cells, m2l_ops, cell_up, cell_down, side_ops):
    coef, ncell = multipoles.shape
    ops = sources.shape[0]
    nhalo = halo_cells.shape[1]
    ngx, ngy, ngz = (mesh.shape[a] for a in AXES)
    nplane = ngx * ngy
    hbm = pl.BlockSpec(memory_space=pltpu.HBM)
    vmem, dma = pltpu.VMEM, pltpu.SemaphoreType.DMA
    m2l = jnp.transpose(m2l_ops, (1, 0, 2)).reshape(coef * ops, coef)
    up = jnp.transpose(cell_up, (1, 0, 2)).reshape(coef * 8, coef)
    down = jnp.transpose(cell_down, (1, 0, 2)).reshape(coef * 8, coef)
    side = jnp.transpose(side_ops, (0, 2, 1, 3))
    return pl.pallas_call(
        functools.partial(kernel, (coef, ncell, ops, nhalo, ngx, ngy, ngz)),
        out_shape=jax.ShapeDtypeStruct((coef, ncell), F32),
        in_specs=[hbm] * 7,
        out_specs=pl.BlockSpec(memory_space=vmem),
        scratch_shapes=[
            vmem((coef, ncell), F32),
            vmem((ncell, 128), F32),
            vmem((ncell + 6 * nhalo, 128), F32),
            vmem((6, nhalo, 128), F32),
            pltpu.SMEM((ops // 8 * (ncell // 128), 8, 128), jnp.int32),
            pltpu.SMEM((6, nhalo), jnp.int32),
            vmem((coef * ops, coef), F32),
            vmem((coef * 8, coef), F32),
            vmem((coef * 8, coef), F32),
            vmem((3, coef, 2, coef), F32),
            vmem((2, 256, 256), BF16),
            vmem((2, 128, 1024), BF16),
            vmem((2, 1024, 128), BF16),
            vmem((3, 2, 128, 128), F32),
            vmem((2, 128, 256), BF16),
            vmem((2, 128, 512), BF16),
            vmem((2, 128, 128 * 16), BF16),
            vmem((ncell, 128), F32),
            vmem((2, 1, 128), F32),
            vmem((ngz, 1, 128), F32),
            vmem((nplane, 1, 128), F32),
            vmem((ngz, 128), F32),
            vmem((16, 128), F32),
            dma((6,)),
            dma((1,)),
            dma((6,)),
            dma((6,)),
            dma((1,)),
            dma((ngz,)),
            dma((1,)),
            dma((1,)),
        ],
        compiler_params=pltpu.CompilerParams(
            collective_id=0, has_side_effects=True, vmem_limit_bytes=63 * 2**20
        ),
        cost_estimate=pl.CostEstimate(flops=3 * 10**9, bytes_accessed=4 * 10**6, transcendentals=0),
    )(multipoles, sources, halo_cells, m2l, up, down, side)


def solution(mesh):
    split_cells = P(None, AXES)
    split_rows = P(AXES, None)
    return jax.shard_map(
        functools.partial(shards, mesh),
        mesh=mesh,
        in_specs=(split_cells, split_rows, split_rows, P(), P(), P(), P()),
        out_specs=split_cells,
        check_vma=False,
    )
```

time: 48.4 us -> 44.7 us (0.924); the launches traced: 47.6 us -> 44.5 us
  Pallas kernels: 45.7 us -> 42.6 us
    pallas_call x1, Pallas kernels: 45.7 us -> 42.6 us  [shards(): pl.pallas_call(functools.partial(kernel, (coef, ncell, ops, nhalo, ngx, n...]
where the time goes in v3:
time: 44.7 us; the launch traced here: 44.5 us
  Pallas kernels  42.6 us (95%)
  local copies, waits for them, and re-layouts  1.89 us (4%)
    pallas_call x1, Pallas kernels, shards(): pl.pallas_call(functools.partial(kernel, (coef, ncell, ops, nhalo, ngx, n...  42.6 us
    unnamed x1, local copies, waits for them, and re-layouts  1.89 us

profile of v3, /device:TPU:480, one launch (start us, length us, event | category | flops | bytes accessed | tf_op | source)
XLA Modules:
  0.0 44.5 jit_solution(17898526261703748561)
XLA Ops:
  0.0 42.6 %shard_map.73 = f32[121,1024]{1,0:T(8,128)} custom-call(f32[121,1024]{1,0:T(8,128)} %mult.1, s32[32,1024]{1,0:T(8,128)} %sources.1, s32[6,256]{1,0:T(8,128)} %halo.1, f32[3872,121]{1,0:T(8,128)} %bitcast.10, f32[968,121]{1,0:T(8,128)} %bitcast.11, f32[968,121]{1,0:T(8,128)} %bitcast.12, f32[3,121,2,121]{3,2,1,0:T(2,128)} %bitcast.13), custom_call_target="tpu_custom_call" | custom-call | flops 3000000000 | bytes 4000000 | tf_op jit(solution)/shard_map/pallas_call | solution.py:387
  42.6 1.9 %copy.9 = f32[121,1024]{1,0:T(8,128)} copy(f32[121,1024]{1,0:T(8,128)} %shard_map.73) | data formatting | bytes 991232

commit v4 on v3

--- a/solution.py
+++ b/solution.py
@@ -12,7 +12,7 @@
 NT = (((1,), (1,)), ((), ()))
 AXES = ("gx", "gy", "gz")
 UP_STEP = 9
-LINE_STEP = 12
+LINE_STEP = 13
 
 
 def split(x):
@@ -63,13 +63,20 @@
     loads = [
         pltpu.make_async_copy(mult, cells, in_sem.at[0]),
         pltpu.make_async_copy(halo, halo_s, in_sem.at[1]),
-        pltpu.make_async_copy(up, up_v, in_sem.at[2]),
         pltpu.make_async_copy(side, side_v, in_sem.at[3]),
-        pltpu.make_async_copy(m2l, m2l_v, in_sem.at[4]),
-        pltpu.make_async_copy(down, down_v, in_sem.at[5]),
     ]
     loads[0].start()
     loads[1].start()
+
+    def slices(table, to, sem):
+        def one(k, c):
+            pltpu.make_async_copy(table.at[:, k, :], to.at[k], in_sem.at[sem]).start()
+            return c
+
+        lax.fori_loop(0, to.shape[0], one, 0)
+
+    def arrive(to, sem):
+        pltpu.make_async_copy(to, to, in_sem.at[sem]).wait()
 
     def source_tile(t):
         g, q = lax.div(t, ncell // 128), lax.rem(t, ncell // 128)
@@ -111,8 +118,10 @@
         own[b * 128 : (b + 1) * 128, :] = block
         pool[b * 128 : (b + 1) * 128, :] = block
 
-    for load in loads[2:]:
-        load.start()
+    slices(up, up_v, 2)
+    loads[2].start()
+    slices(down, down_v, 5)
+    slices(m2l, m2l_v, 4)
     loads[1].wait()
     neighbours = (
         (gx, ngx, lambda i: {"gx": i}),
@@ -175,9 +184,9 @@
 
     for w in (up_w, down_w, side_w, near_w):
         w[...] = jnp.zeros_like(w)
-    loads[2].wait()
+    arrive(up_v, 2)
     for o in range(8):
-        hi, lo = split(up_v[pl.ds(o, coef, 8), :])
+        hi, lo = split(up_v[o])
         up_w[0, 0:coef, o * 128 : o * 128 + coef] = hi
         up_w[1, 0:coef, o * 128 : o * 128 + coef] = lo
 
@@ -191,7 +200,7 @@
     box = dot3(jnp.broadcast_to(flat, (8, 1024)), up_w[0], up_w[1])
     mine[0] = box[0:1, :]
 
-    loads[3].wait()
+    loads[2].wait()
     for a in range(3):
         for b in range(2):
             side_w[a, b, 0:coef, 0:coef] = side_v[a, :, b, :]
@@ -213,9 +222,9 @@
         far_w[0, :, s * 128 : (s + 1) * 128], far_w[1, :, s * 128 : (s + 1) * 128] = split(
             nn3(way[s], cross) if s else cross
         )
-    loads[5].wait()
+    arrive(down_v, 5)
     for o in range(8):
-        hi, lo = split(down_v[pl.ds(o, coef, 8), :])
+        hi, lo = split(down_v[o])
         down_w[0, o * 128 : o * 128 + coef, 0:coef] = hi
         down_w[1, o * 128 : o * 128 + coef, 0:coef] = lo
     acc[...] = jnp.zeros_like(acc)
@@ -314,11 +323,11 @@
 
     def split_near(p, to):
         for h in range(2):
-            hi, lo = split(m2l_v[pl.ds(p * 2 + h, coef, ops), :])
+            hi, lo = split(m2l_v[p * 2 + h])
             near_w[to, 0:coef, h * 128 : h * 128 + coef] = hi
             near_w[to, 128 : 128 + coef, h * 128 : h * 128 + coef] = lo
 
-    loads[4].wait()
+    arrive(m2l_v, 4)
     split_near(0, 0)
 
     def near(p, offs):
@@ -380,9 +389,9 @@
     nplane = ngx * ngy
     hbm = pl.BlockSpec(memory_space=pltpu.HBM)
     vmem, dma = pltpu.VMEM, pltpu.SemaphoreType.DMA
-    m2l = jnp.transpose(m2l_ops, (1, 0, 2)).reshape(coef * ops, coef)
-    up = jnp.transpose(cell_up, (1, 0, 2)).reshape(coef * 8, coef)
-    down = jnp.transpose(cell_down, (1, 0, 2)).reshape(coef * 8, coef)
+    m2l = jnp.transpose(m2l_ops, (1, 0, 2))
+    up = jnp.transpose(cell_up, (1, 0, 2))
+    down = jnp.transpose(cell_down, (1, 0, 2))
     side = jnp.transpose(side_ops, (0, 2, 1, 3))
     return pl.pallas_call(
         functools.partial(kernel, (coef, ncell, ops, nhalo, ngx, ngy, ngz)),
@@ -396,9 +405,9 @@
             vmem((6, nhalo, 128), F32),
             pltpu.SMEM((ops // 8 * (ncell // 128), 8, 128), jnp.int32),
             pltpu.SMEM((6, nhalo), jnp.int32),
-            vmem((coef * ops, coef), F32),
-            vmem((coef * 8, coef), F32),
-            vmem((coef * 8, coef), F32),
+            vmem((ops, coef, coef), F32),
+            vmem((8, coef, coef), F32),
+            vmem((8, coef, coef), F32),
             vmem((3, coef, 2, coef), F32),
             vmem((2, 256, 256), BF16),
             vmem((2, 128, 1024), BF16),

time: 44.7 us -> 42.7 us (0.955)
  Pallas kernels: 42.6 us -> 40.5 us
    pallas_call x1, Pallas kernels: 42.6 us -> 40.5 us  [shards(): pl.pallas_call(functools.partial(kernel, (coef, ncell, ops, nhalo, ngx, n...]
where the time goes in v4:
time: 42.7 us; the launch traced here: 42.4 us
  Pallas kernels  40.5 us (95%)
  local copies, waits for them, and re-layouts  1.89 us (4%)
    pallas_call x1, Pallas kernels, shards(): pl.pallas_call(functools.partial(kernel, (coef, ncell, ops, nhalo, ngx, n...  40.5 us
    unnamed x1, local copies, waits for them, and re-layouts  1.89 us

profile of v4, /device:TPU:480, one launch (start us, length us, event | category | flops | bytes accessed | tf_op | source)
XLA Modules:
  0.0 42.4 jit_solution(12398865622081766354)
XLA Ops:
  0.0 40.5 %shard_map.73 = f32[121,1024]{1,0:T(8,128)} custom-call(f32[121,1024]{1,0:T(8,128)} %mult.1, s32[32,1024]{1,0:T(8,128)} %sources.1, s32[6,256]{1,0:T(8,128)} %halo.1, f32[121,32,121]{2,1,0:T(8,128)} %bitcast.4, f32[121,8,121]{2,1,0:T(8,128)} %bitcast.5, f32[121,8,121]{2,1,0:T(8,128)} %bitcast.6, f32[3,121,2,121]{3,2,1,0:T(2,128)} %bitcast.7), custom_call_target="tpu_custom_call" | custom-call | flops 3000000000 | bytes 4000000 | tf_op jit(solution)/shard_map/pallas_call | solution.py:396
  40.6 1.9 %copy.9 = f32[121,1024]{1,0:T(8,128)} copy(f32[121,1024]{1,0:T(8,128)} %shard_map.73) | data formatting | bytes 991232

commit v5 on v4

--- a/solution.py
+++ b/solution.py
@@ -11,8 +11,8 @@
 MESH = pl.DeviceIdType.MESH
 NT = (((1,), (1,)), ((), ()))
 AXES = ("gx", "gy", "gz")
-UP_STEP = 9
-LINE_STEP = 13
+UP_PAIR = 9
+LINE_PAIR = 12
 
 
 def split(x):
@@ -78,15 +78,8 @@
     def arrive(to, sem):
         pltpu.make_async_copy(to, to, in_sem.at[sem]).wait()
 
-    def source_tile(t):
-        g, q = lax.div(t, ncell // 128), lax.rem(t, ncell // 128)
-        return pltpu.make_async_copy(
-            sources.at[pl.ds(pl.multiple_of(g * 8, 8), 8), pl.ds(pl.multiple_of(q * 128, 128), 128)],
-            src_s.at[t],
-            src_sem.at[0],
-        )
-
-    tiles = ops // 8 * (ncell // 128)
+    def rows_of(k, place):
+        return pltpu.make_async_copy(sources.at[k], src_s[place], src_sem.at[place])
 
     barrier = pltpu.get_barrier_semaphore()
 
@@ -167,23 +160,10 @@
         def _():
             face_copy(2 * a, 2 * a + 1, device(at - 1)).start()
 
-    def fetch(t, c):
-        source_tile(t).start()
-        return c
-
-    lax.fori_loop(0, tiles, fetch, 0)
-
-    for a, (at, count, _) in enumerate(neighbours):
-        @pl.when(at == 0)
-        def _():
-            slot(2 * a)[...] = jnp.zeros((nhalo, 128), F32)
-
-        @pl.when(at == count - 1)
-        def _():
-            slot(2 * a + 1)[...] = jnp.zeros((nhalo, 128), F32)
-
-    for w in (up_w, down_w, side_w, near_w):
-        w[...] = jnp.zeros_like(w)
+    for k in range(4):
+        rows_of(k, k).start()
+
+    up_w[...] = jnp.zeros_like(up_w)
     arrive(up_v, 2)
     for o in range(8):
         hi, lo = split(up_v[o])
@@ -199,6 +179,39 @@
     flat = jnp.concatenate([classes[o : o + 1, :] for o in range(8)], axis=1)
     box = dot3(jnp.broadcast_to(flat, (8, 1024)), up_w[0], up_w[1])
     mine[0] = box[0:1, :]
+
+    def line_copy(sender, device):
+        return pltpu.make_async_remote_copy(
+            src_ref=mine.at[0],
+            dst_ref=line.at[sender],
+            send_sem=line_send.at[0],
+            recv_sem=line_recv.at[sender],
+            device_id={"gz": device},
+            device_id_type=MESH,
+        )
+
+    def send_box(to, c):
+        line_copy(gz, to).start()
+        return c
+
+    def get_box(sender, c):
+        line_copy(sender, sender).wait_recv()
+        return c
+
+    lax.fori_loop(0, gz, send_box, 0)
+    line[gz] = box[0:1, :]
+
+    for a, (at, count, _) in enumerate(neighbours):
+        @pl.when(at == 0)
+        def _():
+            slot(2 * a)[...] = jnp.zeros((nhalo, 128), F32)
+
+        @pl.when(at == count - 1)
+        def _():
+            slot(2 * a + 1)[...] = jnp.zeros((nhalo, 128), F32)
+
+    for w in (down_w, side_w, near_w):
+        w[...] = jnp.zeros_like(w)
 
     loads[2].wait()
     for a in range(3):
@@ -230,24 +243,6 @@
     acc[...] = jnp.zeros_like(acc)
     sibs[...] = jnp.zeros_like(sibs)
 
-    def line_copy(sender, device):
-        return pltpu.make_async_remote_copy(
-            src_ref=mine.at[0],
-            dst_ref=line.at[sender],
-            send_sem=line_send.at[0],
-            recv_sem=line_recv.at[sender],
-            device_id={"gz": device},
-            device_id_type=MESH,
-        )
-
-    def send_box(to, c):
-        line_copy(gz, to).start()
-        return c
-
-    def get_box(sender, c):
-        line_copy(sender, sender).wait_recv()
-        return c
-
     def plane_copy(j):
         return pltpu.make_async_remote_copy(
             src_ref=mine.at[1],
@@ -272,9 +267,6 @@
             device_id=in_plane(1),
             device_id_type=MESH,
         )
-
-    lax.fori_loop(0, gz, send_box, 0)
-    line[gz] = box[0:1, :]
 
     def quads(count):
         rows = [boxes[pl.ds(i, count // 4, 4), :] for i in range(4)]
@@ -319,7 +311,6 @@
             face_copy(2 * a, 2 * a + 1, device(at - 1)).wait_send()
             face_copy(2 * a + 1, 2 * a, device(at - 1)).wait_recv()
 
-    pltpu.make_async_copy(src_s, src_s, src_sem.at[0]).wait()
 
     def split_near(p, to):
         for h in range(2):
@@ -330,33 +321,43 @@
     arrive(m2l_v, 4)
     split_near(0, 0)
 
-    def near(p, offs):
-        @pl.when(p == UP_STEP)
-        def _():
-            lax.fori_loop(gz + 1, ngz, get_box, 0)
-            lax.fori_loop(gz + 1, ngz, send_box, 0)
-
-        pl.when(p == LINE_STEP)(line_done)
-
+    def near_pair(p, half):
         def picked(h, n):
-            v = src_s.at[lax.div(p, 4) * (ncell // 128) + n // 128, lax.rem(p, 4) * 2 + h, pl.ds(n % 128, 8)]
-            return pick8(pool, lambda s: v[offs[s]], sub)
-
-        now = lax.rem(p, 2)
+            return pick8(pool, lambda s: src_s[2 * half + h][n + s], sub)
+
+        for h in range(2):
+            rows_of(2 * p + h, 2 * half + h).wait()
         his, los = [], []
         for n in range(0, ncell, 16):
             rows = [jnp.concatenate([picked(h, n), picked(h, n + 8)], axis=0) for h in range(2)]
             hi, lo = split(jnp.concatenate(rows, axis=1))
             his.append(hi)
             los.append(lo)
-        w = near_w[now]
+
+        @pl.when(p + 2 < ops // 2)
+        def _():
+            for h in range(2):
+                rows_of(2 * p + 4 + h, 2 * half + h).start()
+
+        w = near_w[half]
         both = nt(jnp.concatenate(his, axis=0), w)
         low = nt(jnp.concatenate(los, axis=0), w[0:128])
         acc[...] += both[:, 0:128] + both[:, 128:256] + low
-        split_near(jnp.minimum(p + 1, ops // 2 - 1), 1 - now)
-        return offs
-
-    lax.fori_loop(0, ops // 2, near, offs)
+        split_near(jnp.minimum(p + 1, ops // 2 - 1), 1 - half)
+
+    def hear_above():
+        lax.fori_loop(gz + 1, ngz, get_box, 0)
+        lax.fori_loop(gz + 1, ngz, send_box, 0)
+
+    def near(i, c):
+        for half in range(2):
+            for pair_number, hook in ((UP_PAIR, hear_above), (LINE_PAIR, line_done)):
+                if pair_number % 2 == half:
+                    pl.when(i == pair_number // 2)(hook)
+            near_pair(2 * i + half, half)
+        return c
+
+    lax.fori_loop(0, ops // 4, near, 0)
 
     all_of(plane, nplane, plane_send, plane_recv).wait()
     all_of(line, ngz, line_send, line_recv).wait_send()
@@ -403,7 +404,7 @@
             vmem((ncell, 128), F32),
             vmem((ncell + 6 * nhalo, 128), F32),
             vmem((6, nhalo, 128), F32),
-            pltpu.SMEM((ops // 8 * (ncell // 128), 8, 128), jnp.int32),
+            [pltpu.SMEM((ncell,), jnp.int32)] * 4,
             pltpu.SMEM((6, nhalo), jnp.int32),
             vmem((ops, coef, coef), F32),
             vmem((8, coef, coef), F32),
@@ -423,7 +424,7 @@
             vmem((ngz, 128), F32),
             vmem((16, 128), F32),
             dma((6,)),
-            dma((1,)),
+            dma((4,)),
             dma((6,)),
             dma((6,)),
             dma((1,)),

time: 42.7 us -> 42 us (0.984)
  Pallas kernels: 40.5 us -> 39.9 us
    pallas_call x1, Pallas kernels: 40.5 us -> 39.9 us  [shards(): pl.pallas_call(functools.partial(kernel, (coef, ncell, ops, nhalo, ngx, n...]
where the time goes in v5:
time: 42 us; the launch traced here: 41.8 us
  Pallas kernels  39.9 us (95%)
  local copies, waits for them, and re-layouts  1.89 us (4%)
    pallas_call x1, Pallas kernels, shards(): pl.pallas_call(functools.partial(kernel, (coef, ncell, ops, nhalo, ngx, n...  39.9 us
    unnamed x1, local copies, waits for them, and re-layouts  1.89 us

profile of v5, /device:TPU:480, one launch (start us, length us, event | category | flops | bytes accessed | tf_op | source)
XLA Modules:
  0.0 41.8 jit_solution(13323851710416977999)
XLA Ops:
  0.0 39.9 %shard_map.73 = f32[121,1024]{1,0:T(8,128)} custom-call(f32[121,1024]{1,0:T(8,128)} %mult.1, s32[32,1024]{1,0:T(8,128)} %sources.1, s32[6,256]{1,0:T(8,128)} %halo.1, f32[121,32,121]{2,1,0:T(8,128)} %bitcast.4, f32[121,8,121]{2,1,0:T(8,128)} %bitcast.5, f32[121,8,121]{2,1,0:T(8,128)} %bitcast.6, f32[3,121,2,121]{3,2,1,0:T(2,128)} %bitcast.7), custom_call_target="tpu_custom_call" | custom-call | flops 3000000000 | bytes 4000000 | tf_op jit(solution)/shard_map/pallas_call | solution.py:397
  39.9 1.9 %copy.9 = f32[121,1024]{1,0:T(8,128)} copy(f32[121,1024]{1,0:T(8,128)} %shard_map.73) | data formatting | bytes 991232

commit v6 on v5

--- a/solution.py
+++ b/solution.py
@@ -11,8 +11,8 @@
 MESH = pl.DeviceIdType.MESH
 NT = (((1,), (1,)), ((), ()))
 AXES = ("gx", "gy", "gz")
-UP_PAIR = 9
-LINE_PAIR = 12
+UP_PAIR = 10
+LINE_PAIR = 13
 
 
 def split(x):
@@ -198,7 +198,6 @@
         line_copy(sender, sender).wait_recv()
         return c
 
-    lax.fori_loop(0, gz, send_box, 0)
     line[gz] = box[0:1, :]
 
     for a, (at, count, _) in enumerate(neighbours):
@@ -320,6 +319,8 @@
 
     arrive(m2l_v, 4)
     split_near(0, 0)
+
+    lax.fori_loop(0, gz, send_box, 0)
 
     def near_pair(p, half):
         def picked(h, n):

time: 42 us -> 41.5 us (0.988)
  Pallas kernels: 39.9 us -> 39.4 us
    pallas_call x1, Pallas kernels: 39.9 us -> 39.4 us  [shards(): pl.pallas_call(functools.partial(kernel, (coef, ncell, ops, nhalo, ngx, n...]
where the time goes in v6:
time: 41.5 us; the launch traced here: 41.3 us
  Pallas kernels  39.4 us (95%)
  local copies, waits for them, and re-layouts  1.89 us (5%)
    pallas_call x1, Pallas kernels, shards(): pl.pallas_call(functools.partial(kernel, (coef, ncell, ops, nhalo, ngx, n...  39.4 us
    unnamed x1, local copies, waits for them, and re-layouts  1.89 us

profile of v6, /device:TPU:480, one launch (start us, length us, event | category | flops | bytes accessed | tf_op | source)
XLA Modules:
  0.0 41.3 jit_solution(2610617713164950048)
XLA Ops:
  0.0 39.4 %shard_map.73 = f32[121,1024]{1,0:T(8,128)} custom-call(f32[121,1024]{1,0:T(8,128)} %mult.1, s32[32,1024]{1,0:T(8,128)} %sources.1, s32[6,256]{1,0:T(8,128)} %halo.1, f32[121,32,121]{2,1,0:T(8,128)} %bitcast.4, f32[121,8,121]{2,1,0:T(8,128)} %bitcast.5, f32[121,8,121]{2,1,0:T(8,128)} %bitcast.6, f32[3,121,2,121]{3,2,1,0:T(2,128)} %bitcast.7), custom_call_target="tpu_custom_call" | custom-call | flops 3000000000 | bytes 4000000 | tf_op jit(solution)/shard_map/pallas_call | solution.py:398
  39.5 1.9 %copy.9 = f32[121,1024]{1,0:T(8,128)} copy(f32[121,1024]{1,0:T(8,128)} %shard_map.73) | data formatting | bytes 991232

commit v7 on v6

--- a/solution.py
+++ b/solution.py
@@ -113,8 +113,6 @@
 
     slices(up, up_v, 2)
     loads[2].start()
-    slices(down, down_v, 5)
-    slices(m2l, m2l_v, 4)
     loads[1].wait()
     neighbours = (
         (gx, ngx, lambda i: {"gx": i}),
@@ -160,6 +158,8 @@
         def _():
             face_copy(2 * a, 2 * a + 1, device(at - 1)).start()
 
+    slices(down, down_v, 5)
+    slices(m2l, m2l_v, 4)
     for k in range(4):
         rows_of(k, k).start()
 

time: 41.5 us -> 41.5 us (level)
  no operation moved by 1% of the time
where the time goes in v7:
time: 41.5 us; the launch traced here: 41.3 us
  Pallas kernels  39.4 us (95%)
  local copies, waits for them, and re-layouts  1.89 us (5%)
    pallas_call x1, Pallas kernels, shards(): pl.pallas_call(functools.partial(kernel, (coef, ncell, ops, nhalo, ngx, n...  39.4 us
    unnamed x1, local copies, waits for them, and re-layouts  1.89 us

profile of v7, /device:TPU:480, one launch (start us, length us, event | category | flops | bytes accessed | tf_op | source)
XLA Modules:
  0.0 41.3 jit_solution(11164405815520534535)
XLA Ops:
  0.0 39.4 %shard_map.73 = f32[121,1024]{1,0:T(8,128)} custom-call(f32[121,1024]{1,0:T(8,128)} %mult.1, s32[32,1024]{1,0:T(8,128)} %sources.1, s32[6,256]{1,0:T(8,128)} %halo.1, f32[121,32,121]{2,1,0:T(8,128)} %bitcast.4, f32[121,8,121]{2,1,0:T(8,128)} %bitcast.5, f32[121,8,121]{2,1,0:T(8,128)} %bitcast.6, f32[3,121,2,121]{3,2,1,0:T(2,128)} %bitcast.7), custom_call_target="tpu_custom_call" | custom-call | flops 3000000000 | bytes 4000000 | tf_op jit(solution)/shard_map/pallas_call | solution.py:398
  39.4 1.9 %copy.9 = f32[121,1024]{1,0:T(8,128)} copy(f32[121,1024]{1,0:T(8,128)} %shard_map.73) | data formatting | bytes 991232
